TPU v7x, 256 devices: a whole 4x4x8 slice. The times are simulated.
256 devices in a mesh: ep: 64 (over z, x, core), tp: 4 (over y).
Axes of the slice: x: 4, y: 4, z: 8, core: 2. Of those that a mesh axis runs over, the one named last changes fastest.
Arguments:
- tokens: bfloat16 [1024, 7168], P(('ep', 'tp')), may hold values from -6 to 6
- expert_ids: int32 [1024, 8], P(('ep', 'tp')), may hold values from 0 to 31, all different within a row; in each aligned block of 4 rows (0 to 3, 4 to 7, ...) at most 2 rows name the same one
- affinity: float32 [1024, 8], P(('ep', 'tp')), may hold values from 0.1 to 1
- gate_weight: bfloat16 [64, 7168, 1024], P('ep', None, 'tp'), may hold values from -0.0625 to 0.0625
- up_weight: bfloat16 [64, 7168, 1024], P('ep', None, 'tp'), may hold values from -0.0625 to 0.0625
- down_weight: bfloat16 [64, 1024, 7168], P('ep', 'tp'), may hold values from -0.125 to 0.125
Outputs:
- mixed: bfloat16 [1024, 7168], P(('ep', 'tp'))
Inputs may be any that keep to these rules, and one draw needn't show every extreme that they name: `expert_ids`: each row names 8 different experts. Among the 4 rows of one device no expert is named by more than 2 rows, and some device's rows name one expert exactly 2 times.
All inputs are finite; a program needn't handle non-finite values.
Results may differ from a plain program's by a relative error of at most 0.0065.
Values may be sent and summed in bfloat16 or wider, within the bound.
No kernel may reach another device: no remote copies, remote signals or barrier semaphores. Data moves between devices by JAX's collectives and lax.ppermute only.
A program may use at most 128 MiB of HBM per device.

v0:
```python
import jax
import jax.numpy as jnp
from jax import lax
from jax.sharding import PartitionSpec as P


def hidden_of(piece_rows, gate_local, up_local):
    gate_value = jnp.dot(piece_rows, gate_local, preferred_element_type=jnp.float32)
    up_value = jnp.dot(piece_rows, up_local, preferred_element_type=jnp.float32)
    return (jax.nn.silu(gate_value) * up_value).astype(jnp.bfloat16)


def expert_half(rows_in, gate_local, up_local, down_local):
    partials = jnp.dot(
        hidden_of(lax.all_gather(rows_in, "tp", axis=0, tiled=True), gate_local, up_local),
        down_local,
        preferred_element_type=jnp.float32,
    )
    return lax.psum_scatter(partials, "tp", scatter_dimension=0, tiled=True).astype(jnp.bfloat16)


def shards(tokens, expert_ids, affinity, gate_weight, up_weight, down_weight):
    ep_count = lax.axis_size("ep")
    experts = ep_count // 2
    tok_count = tokens.shape[0]
    model_width = tokens.shape[1]
    top_count = expert_ids.shape[1]
    slot_count = 2 * max(1, tok_count * top_count // experts)
    gate_local = gate_weight[0]
    up_local = up_weight[0]
    down_local = down_weight[0]
    weights = 2.5 * affinity / jnp.sum(affinity, axis=1, keepdims=True)
    labels = jnp.arange(experts, dtype=jnp.int32)
    matches = (expert_ids[:, :, None] == labels[None, None, :]).astype(jnp.float32)
    chosen = jnp.sum(matches, axis=1)
    shares = jnp.sum(matches * weights[:, :, None], axis=1)
    earlier = jnp.cumsum(chosen, axis=0) - chosen
    slot_values = jnp.arange(slot_count, dtype=jnp.float32)
    picked = chosen.T[:, None, :] * (earlier.T[:, None, :] == slot_values[None, :, None]).astype(
        jnp.float32
    )
    routing = jnp.repeat(picked, 2, axis=0)
    outgoing = jnp.einsum(
        "ist,td->isd", routing.astype(jnp.bfloat16), tokens, preferred_element_type=jnp.float32
    ).astype(jnp.bfloat16)
    arrived = lax.all_to_all(outgoing, "ep", split_axis=0, concat_axis=0, tiled=True)
    half_rows = expert_half(arrived.reshape(-1, model_width), gate_local, up_local, down_local)
    returned = lax.all_to_all(
        half_rows.reshape(ep_count, slot_count, model_width),
        "ep",
        split_axis=0,
        concat_axis=0,
        tiled=True,
    )
    paired = jnp.sum(
        returned.reshape(experts, 2, slot_count, model_width).astype(jnp.float32), axis=1
    )
    expert_output = lax.optimization_barrier(paired.astype(jnp.bfloat16)).astype(jnp.float32)
    expert_output = expert_output.reshape(experts * slot_count, model_width)
    coefficients = (picked * shares.T[:, None, :]).reshape(experts * slot_count, tok_count)
    mixed = jnp.dot(
        coefficients.T,
        expert_output,
        precision=lax.Precision.HIGHEST,
        preferred_element_type=jnp.float32,
    )
    return mixed.astype(jnp.bfloat16)


def solution(mesh):
    return jax.shard_map(
        shards,
        mesh=mesh,
        in_specs=(
            P(("ep", "tp"), None),
            P(("ep", "tp"), None),
            P(("ep", "tp"), None),
            P("ep", None, "tp"),
            P("ep", None, "tp"),
            P("ep", "tp", None),
        ),
        out_specs=P(("ep", "tp"), None),
        check_vma=False,
    )
```

profile of v0, /device:TPU:2, one launch (start us, length us, event | category | flops | bytes accessed | tf_op | source)
XLA Modules:
  0.0 377.4 jit_solution(4780029797709461180)
XLA Ops:
  6.5 0.0 copy-start
  6.5 0.0 all-gather.2.cloned.1.call-start
  6.5 0.8 reduce_sum.43
  7.4 0.8 multiply_divide_fusion
  8.1 0.8 select_reduce_fusion
  8.9 0.1 copy.14
  9.1 0.0 copy-done
  9.1 0.6 convolution_convert_fusion
  9.7 1.9 copy.16
  11.6 57.5 %all_to_all.10 = bf16[64,2,7168]{2,1,0:T(2,128)(2,1)S(1)} all-to-all(bf16[64,2,7168]{2,1,0:T(2,128)(2,1)S(1)} %copy.16), channel_id=1, replica_groups=mesh['ep'=64,'tp'=4] {'ep'}, dimensions={0} | all-to-all | bytes 3670016 | tf_op jit(solution)/shard_map/all_to_all | solution.py:46
  69.0 1.7 reshape.19
  70.7 0.0 all-gather.2.cloned.1.call-update
  70.7 0.2 reduce-scatter.2.cloned.1.call-start
  71.0 73.3 %all-gather.2.cloned.1.call-done = bf16[512,7168]{1,0:T(8,128)(2,1)} async-done(((bf16[128,7168]{1,0:T(8,128)(2,1)}), bf16[512,7168]{1,0:T(8,128)(2,1)}) %all-gather.2.cloned.1.call-update) | async-done | bytes 7340048 | tf_op jit(solution)/shard_map/all_gather | solution.py:15
  144.3 6.2 %fusion.5 = f32[512,256]{1,0:T(8,128)S(1)} fusion(bf16[512,7168]{1,0:T(8,128)(2,1)} %all-gather.2.cloned.1.call-done, bf16[1,7168,256]{2,1,0:T(8,128)(2,1)} %param.9), kind=kOutput, calls=%fused_computation.7 | convolution fusion | flops 1879048192 | bytes 11534336 | tf_op jit(solution)/shard_map/dot_general | solution.py:8
  150.4 18.2 %fusion.1 = f32[512,7168]{1,0:T(8,128)} fusion(bf16[1,256,7168]{2,1,0:T(8,128)(2,1)} %param.11, bf16[512,7168]{1,0:T(8,128)(2,1)} %all-gather.2.cloned.1.call-done, bf16[1,7168,256]{2,1,0:T(8,128)(2,1)} %param.10, f32[512,256]{1,0:T(8,128)S(1)} %fusion.5), kind=kOutput, calls=%fused_computation.3 | convolution fusion | flops 3758882816 | bytes 29884416 | tf_op jit(solution)/shard_map/dot_general | solution.py:14
  168.6 0.0 reduce-scatter.2.cloned.1.call-update
  168.7 135.0 %reduce-scatter.2.cloned.1.call-done = f32[128,7168]{1,0:T(8,128)} async-done(((f32[512,7168]{1,0:T(8,128)}), f32[128,7168]{1,0:T(8,128)}) %reduce-scatter.2.cloned.1.call-update) | async-done | bytes 3670032 | tf_op jit(solution)/shard_map/reduce_scatter | solution.py:19
  303.7 3.5 convert_element_type.31
  307.2 3.9 %reshape.20 = bf16[64,2,7168]{2,1,0:T(2,128)(2,1)S(1)} reshape(bf16[128,7168]{1,0:T(8,128)(2,1)} %convert_element_type.31) | data formatting | bytes 3670016 | tf_op jit(solution)/shard_map/reshape | solution.py:49
  311.1 56.0 %all_to_all.11 = bf16[64,2,7168]{2,1,0:T(2,128)(2,1)S(1)} all-to-all(bf16[64,2,7168]{2,1,0:T(2,128)(2,1)S(1)} %reshape.20), channel_id=1, replica_groups=mesh['ep'=64,'tp'=4] {'ep'}, dimensions={0} | all-to-all | bytes 3670016 | tf_op jit(solution)/shard_map/all_to_all | solution.py:48
  367.1 2.3 bitcast_reduce_fusion
  369.4 1.2 fusion
  (4 shorter events, 0.1 us)
Async XLA Ops:
  6.5 2.5 copy-start
  6.5 137.7 %all-gather.2.cloned.1.call-start = ((), (), s32[]{:S(2)}) async-start(), calls=%async_computation.3 | async-start | bytes 9175040 | tf_op jit(solution)/shard_map/all_gather | solution.py:15
  70.7 233.0 %reduce-scatter.2.cloned.1.call-start = ((), (), s32[]{:S(2)}) async-start(), calls=%async_computation.4 | async-start | bytes 18350080 | tf_op jit(solution)/shard_map/reduce_scatter | solution.py:19
Sparse Core Ops, SparseCore 0:
  70.9 73.3 all-gather.1
  168.8 134.8 reduce-scatter.1
where the time goes:
time: 378 us; the launch traced here: 377 us
  waiting for transfers between devices  208 us (55%)
  blocking collectives  113 us (30%)
  matrix products  26.2 us (7%)
  between operations  13.5 us (4%)
  other arithmetic  8.2 us (2%)
  local copies, waits for them, and re-layouts  7.57 us (2%)
    reduce_scatter x1, waiting for transfers between devices, expert_half(): lax.psum_scatter(partials, 'tp', scatter_dimension=0, tiled=True)  135 us
    all_gather x1, waiting for transfers between devices, expert_half(): lax.all_gather(rows_in, 'tp', axis=0, tiled=True)  73.3 us
    all_to_all x1, blocking collectives, shards(): lax.all_to_all(outgoing, 'ep', split_axis=0, concat_axis=0, tiled=True)  57.5 us
    all_to_all x1, blocking collectives, shards(): lax.all_to_all(half_rows.reshape(ep_count, slot_count, model_width), 'ep'...  56 us
    dot_general x1, matrix products, expert_half(): jnp.dot(hidden_of(lax.all_gather(rows_in, 'tp', axis=0, tiled=True), gate...  18.2 us
  transfers between devices with their start and end apart: 2, of which 2 were waited for; matrix products, arithmetic and copies ran while one was open for 0% of the time, Pallas kernels for 0%

commit v1 on v0

v1 whole, which is shorter than its diff:
```python
import functools

import jax
import jax.numpy as jnp
from jax import lax
from jax.experimental import pallas as pl
from jax.experimental.pallas import tpu as pltpu
from jax.sharding import PartitionSpec as P

MIB = 1024 * 1024
WAIT = 256 * MIB
PART = 32
ANYWHERE = pl.BlockSpec(memory_space=pl.ANY)
ONCHIP = pl.BlockSpec(memory_space=pltpu.VMEM)


def after(values, *first, cost=0):
    return pl.pallas_call(
        lambda *refs: None,
        in_specs=[ANYWHERE] * (len(values) + len(first)),
        out_specs=[ANYWHERE] * len(values),
        out_shape=[jax.ShapeDtypeStruct(value.shape, value.dtype) for value in values],
        input_output_aliases={place: place for place in range(len(values))},
        compiler_params=pltpu.CompilerParams(vmem_limit_bytes=MIB),
        cost_estimate=pl.CostEstimate(flops=0, bytes_accessed=cost, transcendentals=0),
    )(*values, *first)


def stage_kernel(*refs):
    half = len(refs) // 3
    copies = [
        pltpu.make_async_copy(refs[place], refs[half + place], refs[2 * half + place])
        for place in range(half)
    ]
    for copy in copies:
        copy.start()
    for copy in copies:
        copy.wait()


def stage(*weights):
    return pl.pallas_call(
        stage_kernel,
        in_specs=[pl.BlockSpec(memory_space=pltpu.HBM)] * len(weights),
        out_specs=[ONCHIP] * len(weights),
        out_shape=[pltpu.VMEM(weight.shape, weight.dtype) for weight in weights],
        scratch_shapes=[pltpu.SemaphoreType.DMA] * len(weights),
        compiler_params=pltpu.CompilerParams(vmem_limit_bytes=MIB),
    )(*weights)


def ffn_kernel(pieces, tiles, *refs):
    own_refs, refs = refs[:pieces], refs[pieces:]
    other_refs, refs = refs[:pieces], refs[pieces:]
    gate_ref, up_ref, down_ref, keep_ref, *send_refs = refs
    half, width = keep_ref.shape
    part = half // len(send_refs)
    rows = jnp.concatenate([ref[...] for ref in (*own_refs, *other_refs)], axis=0)
    gate_value = jnp.dot(rows, gate_ref[0], preferred_element_type=jnp.float32)
    up_value = jnp.dot(rows, up_ref[0], preferred_element_type=jnp.float32)
    hidden = gate_value / (1.0 + jnp.exp(-gate_value)) * up_value
    hidden = hidden.astype(jnp.bfloat16)
    for tile in range(tiles):
        span = slice(tile * (width // tiles), (tile + 1) * (width // tiles))
        out = jnp.dot(hidden, down_ref[0, :, span], preferred_element_type=jnp.float32)
        keep_ref[:, span] = out[:half].astype(jnp.bfloat16)
        for place, send_ref in enumerate(send_refs):
            first = half + place * part
            send_ref[:, span] = out[first : first + part].astype(jnp.bfloat16)


def ffn(own, other, gate_weight, up_weight, down_weight):
    half = sum(piece.shape[0] for piece in own)
    width = own[0].shape[1]
    units = gate_weight.shape[2]
    parts = half // PART
    return pl.pallas_call(
        functools.partial(ffn_kernel, len(own), 4),
        in_specs=[ONCHIP] * (2 * len(own) + 3),
        out_specs=[ONCHIP] * (1 + parts),
        out_shape=[jax.ShapeDtypeStruct((half, width), jnp.bfloat16)]
        + [jax.ShapeDtypeStruct((PART, width), jnp.bfloat16)] * parts,
        compiler_params=pltpu.CompilerParams(vmem_limit_bytes=16 * MIB),
        cost_estimate=pl.CostEstimate(
            flops=2 * 2 * half * 3 * width * units,
            bytes_accessed=3 * width * units * 2 + half * width * 8,
            transcendentals=2 * half * units,
        ),
    )(*own, *other, gate_weight, up_weight, down_weight)


def shards(tokens, expert_ids, affinity, gate_weight, up_weight, down_weight):
    ep_count = lax.axis_size("ep")
    tp_count = lax.axis_size("tp")
    experts = ep_count // 2
    tok_count, width = tokens.shape
    top_count = expert_ids.shape[1]
    slots = 2 * max(1, tok_count * top_count // experts)
    count = experts * slots
    half = count // 2
    same_core = [[i for i in range(ep_count) if i % 2 == c] for c in range(2)]

    def over_core(value):
        return lax.ppermute(value, "ep", [(i, i ^ 1) for i in range(ep_count)])

    def over_y(value, shift):
        return lax.ppermute(
            value, "tp", [(i, (i + shift) % tp_count) for i in range(tp_count)]
        )

    def exchange(value):
        return lax.all_to_all(
            value, "ep", split_axis=0, concat_axis=0, axis_index_groups=same_core, tiled=True
        )

    def wide(value):
        return value.astype(jnp.float32)

    def narrow(value):
        return value.astype(jnp.bfloat16)

    weights = 2.5 * affinity / jnp.sum(affinity, axis=1, keepdims=True)
    labels = jnp.arange(experts, dtype=jnp.int32)
    matches = (expert_ids[:, :, None] == labels[None, None, :]).astype(jnp.float32)
    chosen = jnp.sum(matches, axis=1)
    shares = jnp.sum(matches * weights[:, :, None], axis=1)
    earlier = jnp.cumsum(chosen, axis=0) - chosen
    slot_values = jnp.arange(slots, dtype=jnp.float32)
    picked = chosen.T[:, None, :] * (earlier.T[:, None, :] == slot_values[None, :, None]).astype(
        jnp.float32
    )
    picked = picked.reshape(count, tok_count)
    coefficients = picked * jnp.repeat(shares.T, slots, axis=0)
    outgoing = narrow(
        jnp.dot(picked.astype(jnp.bfloat16), tokens, preferred_element_type=jnp.float32)
    )

    staged = stage(gate_weight, up_weight, down_weight)

    own = exchange(outgoing)
    left, right = over_y(own, 1), over_y(own, -1)
    own_kept, *own_sent = ffn([own], [over_core(own)], *staged)
    left, right = after([left, right], own_kept)

    far = [over_y(left[:half], 1), over_y(right[half:], -1)]
    near = [left, right]
    near_kept, *near_sent = ffn(near, [over_core(piece) for piece in near], *staged)
    far = after(far, near_kept, cost=WAIT)
    *near_got, far_low = after([*map(over_core, near_sent), far[0]], far[1])
    far = [far_low, far[1]]
    near_sum = [
        wide(near_kept[place * half : (place + 1) * half]) + wide(got)
        for place, got in enumerate(near_got)
    ]

    to_left, to_right = over_y(narrow(near_sum[0]), -1), over_y(narrow(near_sum[3]), 1)
    far_kept, *far_sent = ffn(far, [over_core(piece) for piece in far], *staged)
    to_left, to_right = after([to_left, to_right], far_kept, cost=WAIT)
    far_got = after([*map(over_core, far_sent)], to_left, to_right)

    passed_right = over_y(narrow(wide(far_kept[:half]) + wide(far_got[0])), 1)
    passed_left = over_y(narrow(wide(far_kept[half:]) + wide(far_got[1])), -1)
    last_right = over_y(narrow(near_sum[2] + wide(passed_right)), 1)
    last_left = over_y(narrow(near_sum[1] + wide(passed_left)), -1)
    own_got = jnp.concatenate([over_core(piece) for piece in own_sent], axis=0)
    from_left = wide(jnp.concatenate([last_right, to_right], axis=0))
    from_right = wide(jnp.concatenate([to_left, last_left], axis=0))
    own_total = wide(own_kept) + wide(own_got)
    returned = exchange(narrow(own_total + from_left + from_right))
    mixed = jnp.dot(
        coefficients.T,
        wide(returned),
        precision=lax.Precision.HIGHEST,
        preferred_element_type=jnp.float32,
    )
    return narrow(mixed)


def solution(mesh):
    return jax.shard_map(
        shards,
        mesh=mesh,
        in_specs=(
            P(("ep", "tp"), None),
            P(("ep", "tp"), None),
            P(("ep", "tp"), None),
            P("ep", None, "tp"),
            P("ep", None, "tp"),
            P("ep", "tp", None),
        ),
        out_specs=P(("ep", "tp"), None),
        check_vma=False,
    )
```

time: 378 us -> 154 us (0.41)
  waiting for transfers between devices: 208 us -> 72.8 us
  blocking collectives: 113 us -> 36.7 us
  matrix products: 26.2 us -> 1.61 us
  starting transfers between devices: 0.22 us -> 22.7 us
  between operations: 13.5 us -> 0.19 us
  Pallas kernels: 0 us -> 7.53 us
  other arithmetic: 8.2 us -> 3.62 us
    reduce_scatter x1 -> x0, waiting for transfers between devices: 135 us -> none  [expert_half(): lax.psum_scatter(partials, 'tp', scatter_dimension=0, tiled=True)]
    all_to_all x2 -> x1, blocking collectives: 113 us -> 36.7 us  [exchange(): lax.all_to_all(value, 'ep', split_axis=0, concat_axis=0, axis_index_group...]
    all_gather x1 -> x0, waiting for transfers between devices: 73.3 us -> none  [expert_half(): lax.all_gather(rows_in, 'tp', axis=0, tiled=True)]
    ppermute x0 -> x23, waiting for transfers between devices: none -> 50.2 us  [the longest x10 48.8 us: over_y(): lax.ppermute(value, 'tp', [(i, (i + shift) % tp_count) for i in range(tp_...]
    dot_general x4 -> x2, matrix products: 26.2 us -> 1.61 us  [the longest x1 1.17 us: shards(): jnp.dot(coefficients.T, wide(returned), precision=lax.Precision.HIGHEST,...]
    all_to_all x0 -> x1, waiting for transfers between devices: none -> 22.7 us  [exchange(): lax.all_to_all(value, 'ep', split_axis=0, concat_axis=0, axis_index_group...]
    ppermute x0 -> x23, starting transfers between devices: none -> 17.1 us  [the longest x10 14.2 us: over_y(): lax.ppermute(value, 'tp', [(i, (i + shift) % tp_count) for i in range(tp_...]
    pallas_call x0 -> x9, Pallas kernels: none -> 7.53 us  [the longest x3 6.77 us: ffn(): pl.pallas_call(functools.partial(ffn_kernel, len(own), 4), in_specs=[ONCH...]
  transfers between devices with their start and end apart: 2 -> 24, of which waited for: 2 -> 10; matrix products, arithmetic and copies ran while one was open for 0% -> 0% of each run, Pallas kernels for 0% -> 5%
where the time goes in v1:
time: 154 us
  waiting for transfers between devices  72.8 us (47%)
  blocking collectives  36.7 us (24%)
  starting transfers between devices  22.7 us (15%)
  local copies, waits for them, and re-layouts  8.57 us (6%)
  Pallas kernels  7.53 us (5%)
  other arithmetic  3.62 us (2%)
  matrix products  1.61 us (1%)
    ppermute x10, waiting for transfers between devices, over_y(): lax.ppermute(value, 'tp', [(i, (i + shift) % tp_count) for i in range(tp_...  48.8 us
    all_to_all x1, blocking collectives, exchange(): lax.all_to_all(value, 'ep', split_axis=0, concat_axis=0, axis_index_group...  36.7 us
    all_to_all x1, waiting for transfers between devices, exchange(): lax.all_to_all(value, 'ep', split_axis=0, concat_axis=0, axis_index_group...  22.7 us
    ppermute x10, starting transfers between devices, over_y(): lax.ppermute(value, 'tp', [(i, (i + shift) % tp_count) for i in range(tp_...  14.2 us
    pallas_call x3, Pallas kernels, ffn(): pl.pallas_call(functools.partial(ffn_kernel, len(own), 4), in_specs=[ONCH...  6.77 us
    unnamed x8, local copies, waits for them, and re-layouts  6.12 us
    all_to_all x1, starting transfers between devices, exchange(): lax.all_to_all(value, 'ep', split_axis=0, concat_axis=0, axis_index_group...  5.57 us
  transfers between devices with their start and end apart: 24, of which 10 were waited for; matrix products, arithmetic and copies ran while one was open for 0% of the time, Pallas kernels for 5%

profile of v1, /device:TPU:2, one launch (start us, length us, event | category | flops | bytes accessed | tf_op | source)
XLA Modules:
  0.0 153.7 jit_solution(10796258208916155197)
XLA Ops:
  0.0 0.8 reduce_sum.31
  0.8 0.8 multiply_divide_fusion
  1.6 0.8 select_reduce_fusion
  2.6 0.1 eq.46
  2.7 0.4 convolution_convert_fusion
  3.2 0.3 all_to_all.13
  3.5 36.7 %all_to_all.20 = bf16[32,2,7168]{2,1,0:T(2,128)(2,1)S(1)} all-to-all(bf16[32,2,7168]{2,1,0:T(2,128)(2,1)S(1)} %all_to_all.13), channel_id=1, replica_groups={{0,8,16,24,32,40,48,56,64,72,80,88,96,104,112,120,128,136,144,152,160,1..., dimensions={0} | all-to-all | bytes 1835008 | tf_op jit(solution)/shard_map/all_to_all | solution.py:112
  40.2 0.3 all_to_all.15.refs_0_
  40.6 1.7 %collective-permute-start.3 = (bf16[64,7168]{1,0:T(8,128)(2,1)S(1)}, bf16[64,7168]{1,0:T(8,128)(2,1)S(1)}, u32[]{:S(2)}, u32[]{:S(2)}) collective-permute-start(bf16[64,7168]{1,0:T(8,128)(2,1)S(1)} %all_to_all.15.refs_0_), channel_id=1, source_target_pairs={{0,1},{1,2},{2,3},{3,0},{4,5},{5,6},{6,7},{7,4},{8,9},{9,10},{10,1... | collective-permute-start | bytes 2752520 | tf_op jit(solution)/shard_map/ppermute | solution.py:107
  42.3 1.7 %collective-permute-start.4 = (bf16[64,7168]{1,0:T(8,128)(2,1)S(1)}, bf16[64,7168]{1,0:T(8,128)(2,1)S(1)}, u32[]{:S(2)}, u32[]{:S(2)}) collective-permute-start(bf16[64,7168]{1,0:T(8,128)(2,1)S(1)} %all_to_all.15.refs_0_), channel_id=1, source_target_pairs={{0,3},{1,0},{2,1},{3,2},{4,7},{5,4},{6,5},{7,6},{8,11},{9,8},{10,9... | collective-permute-start | bytes 2752520 | tf_op jit(solution)/shard_map/ppermute | solution.py:107
  44.0 2.0 %copy-done.1 = bf16[1,7168,256]{2,1,0:T(8,128)(2,1)S(1)} copy-done((bf16[1,7168,256]{2,1,0:T(8,128)(2,1)S(1)}, bf16[1,7168,256]{2,1,0:T(8,128)(2,1)}, u32[]{:S(2)}) %copy-start.1) | copy-done | bytes 3670040
  46.0 2.0 %copy-done.2 = bf16[1,7168,256]{2,1,0:T(8,128)(2,1)S(1)} copy-done((bf16[1,7168,256]{2,1,0:T(8,128)(2,1)S(1)}, bf16[1,7168,256]{2,1,0:T(8,128)(2,1)}, u32[]{:S(2)}) %copy-start.2) | copy-done | bytes 3670040
  48.0 2.0 %copy-done.3 = bf16[1,256,7168]{2,1,0:T(8,128)(2,1)S(1)} copy-done((bf16[1,256,7168]{2,1,0:T(8,128)(2,1)S(1)}, bf16[1,256,7168]{2,1,0:T(8,128)(2,1)}, u32[]{:S(2)}) %copy-start.3) | copy-done | bytes 3670040
  50.1 0.8 shard_map.64
  50.9 1.8 %shard_map.65 = (bf16[64,7168]{1,0:T(8,128)(2,1)S(1)}, bf16[32,7168]{1,0:T(8,128)(2,1)S(1)}, bf16[32,7168]{1,0:T(8,128)(2,1)S(1)}) custom-call(bf16[64,7168]{1,0:T(8,128)(2,1)S(1)} %all_to_all.15.refs_0_, bf16[64,7168]{1,0:T(8,128)(2,1)S(1)} %collective-permute-done.refs_1_, bf16[1,7168,256]{2,1,0:T(8,128)(2,1)S(1)} %get-tuple-element.32.refs_2_.refs_4_, ...), custom_call_target="tpu_custom_call" | custom-call | flops 1409286144 | bytes 14680064 | tf_op jit(solution)/shard_map/pallas_call | solution.py:77
  52.7 12.0 %collective-permute-done.3.refs_0_ = bf16[64,7168]{1,0:T(8,128)(2,1)S(1)} collective-permute-done((bf16[64,7168]{1,0:T(8,128)(2,1)S(1)}, bf16[64,7168]{1,0:T(8,128)(2,1)S(1)}, u32[]{:S(2)}, u32[]{:S(2)}) %collective-permute-start.3) | collective-permute-done | bytes 917536 | tf_op jit(solution)/shard_map/ppermute | solution.py:107
  64.7 0.5 collective-permute-start.6
  65.2 1.7 %collective-permute-start.11 = (bf16[32,7168]{1,0:T(8,128)(2,1)S(1)}, bf16[32,7168]{1,0:T(8,128)(2,1)S(1)}, u32[]{:S(2)}, u32[]{:S(2)}) collective-permute-start(bf16[32,7168]{1,0:T(8,128)(2,1)S(1)} %slice.25), channel_id=1, source_target_pairs={{0,1},{1,2},{2,3},{3,0},{4,5},{5,6},{6,7},{7,4},{8,9},{9,10},{10,1... | collective-permute-start | bytes 1376264 | tf_op jit(solution)/shard_map/ppermute | solution.py:107
  66.9 1.7 %collective-permute-start.12 = (bf16[32,7168]{1,0:T(8,128)(2,1)S(1)}, bf16[32,7168]{1,0:T(8,128)(2,1)S(1)}, u32[]{:S(2)}, u32[]{:S(2)}) collective-permute-start(bf16[32,7168]{1,0:T(8,128)(2,1)S(1)} %slice.26), channel_id=1, source_target_pairs={{0,3},{1,0},{2,1},{3,2},{4,7},{5,4},{6,5},{7,6},{8,11},{9,8},{10,9... | collective-permute-start | bytes 1376264 | tf_op jit(solution)/shard_map/ppermute | solution.py:107
  68.7 3.2 %shard_map.67 = (bf16[128,7168]{1,0:T(8,128)(2,1)S(1)}, bf16[32,7168]{1,0:T(8,128)(2,1)S(1)}, bf16[32,7168]{1,0:T(8,128)(2,1)S(1)}, bf16[32,7168]{1,0:T(8,128)(2,1)S(1)}, bf16[32,7168]{1,0:T(8,128)(2,1)S(1)}) custom-call(bf16[64,7168]{1,0:T(8,128)(2,1)S(1)} %get-tuple-element.38.refs_0_, bf16[64,7168]{1,0:T(8,128)(2,1)S(1)} %get-tuple-element.39.refs_1_, ...), custom_call_target="tpu_custom_call" | custom-call | flops 2818572288 | bytes 18350080 | tf_op jit(solution)/shard_map/pallas_call | solution.py:77
  72.0 0.5 collective-permute-start.8
  72.6 6.4 %collective-permute-done.11.refs_0_ = bf16[32,7168]{1,0:T(8,128)(2,1)S(1)} collective-permute-done((bf16[32,7168]{1,0:T(8,128)(2,1)S(1)}, bf16[32,7168]{1,0:T(8,128)(2,1)S(1)}, u32[]{:S(2)}, u32[]{:S(2)}) %collective-permute-start.11) | collective-permute-done | bytes 458784 | tf_op jit(solution)/shard_map/ppermute | solution.py:107
  79.0 0.1 collective-permute-done.12.refs_1_
  79.2 0.4 collective-permute-start.14
  79.5 1.3 collective-permute-done.10.refs_3_
  80.8 0.1 collective-permute-start.13
  81.0 0.2 add_convert_fusion.5
  81.2 1.8 %collective-permute-start.17 = (bf16[32,7168]{1,0:T(8,128)(2,1)S(1)}, bf16[32,7168]{1,0:T(8,128)(2,1)S(1)}, u32[]{:S(2)}, u32[]{:S(2)}) collective-permute-start(bf16[32,7168]{1,0:T(8,128)(2,1)S(1)} %get-tuple-element.64), channel_id=1, source_target_pairs={{0,3},{1,0},{2,1},{3,2},{4,7},{5,4},{6,5},{7,6},{8,11},{9,8},{10,9... | collective-permute-start | bytes 1376264 | tf_op jit(solution)/shard_map/ppermute | solution.py:107
  83.0 0.3 collective-permute-start.18
  83.3 1.8 %shard_map.70 = (bf16[64,7168]{1,0:T(8,128)(2,1)S(1)}, bf16[32,7168]{1,0:T(8,128)(2,1)S(1)}, bf16[32,7168]{1,0:T(8,128)(2,1)S(1)}) custom-call(bf16[32,7168]{1,0:T(8,128)(2,1)S(1)} %get-tuple-element.48.refs_0_, bf16[32,7168]{1,0:T(8,128)(2,1)S(1)} %get-tuple-element.46.refs_5_.refs_1_, bf16[32,7168]{1,0:T(8,128)(2,1)S(1)} %collective-permute-done.13.refs_2_, ...), custom_call_target="tpu_custom_call" | custom-call | flops 1409286144 | bytes 14680064 | tf_op jit(solution)/shard_map/pallas_call | solution.py:77
  85.2 0.5 collective-permute-start.16
  85.7 8.4 %collective-permute-done.17.refs_0_ = bf16[32,7168]{1,0:T(8,128)(2,1)S(1)} collective-permute-done((bf16[32,7168]{1,0:T(8,128)(2,1)S(1)}, bf16[32,7168]{1,0:T(8,128)(2,1)S(1)}, u32[]{:S(2)}, u32[]{:S(2)}) %collective-permute-start.17) | collective-permute-done | bytes 458784 | tf_op jit(solution)/shard_map/ppermute | solution.py:107
  94.1 2.6 %collective-permute-done.18.refs_1_ = bf16[32,7168]{1,0:T(8,128)(2,1)S(1)} collective-permute-done((bf16[32,7168]{1,0:T(8,128)(2,1)S(1)}, bf16[32,7168]{1,0:T(8,128)(2,1)S(1)}, u32[]{:S(2)}, u32[]{:S(2)}) %collective-permute-start.18) | collective-permute-done | bytes 458784 | tf_op jit(solution)/shard_map/ppermute | solution.py:107
  96.7 0.2 add_convert_fusion.2
  96.9 0.4 collective-permute-start.21
  97.2 1.7 %collective-permute-start.19 = (bf16[32,7168]{1,0:T(8,128)(2,1)S(1)}, bf16[32,7168]{1,0:T(8,128)(2,1)S(1)}, u32[]{:S(2)}, u32[]{:S(2)}) collective-permute-start(bf16[32,7168]{1,0:T(8,128)(2,1)S(1)} %get-tuple-element.66), channel_id=1, source_target_pairs={{0,1},{1,2},{2,3},{3,0},{4,5},{5,6},{6,7},{7,4},{8,9},{9,10},{10,1... | collective-permute-start | bytes 1376264 | tf_op jit(solution)/shard_map/ppermute | solution.py:107
  99.0 0.5 collective-permute-start.1
  99.5 9.0 %collective-permute-done.21 = bf16[32,7168]{1,0:T(8,128)(2,1)S(1)} collective-permute-done((bf16[32,7168]{1,0:T(8,128)(2,1)S(1)}, bf16[32,7168]{1,0:T(8,128)(2,1)S(1)}, u32[]{:S(2)}, u32[]{:S(2)}) %collective-permute-start.21) | collective-permute-done | bytes 458784 | tf_op jit(solution)/shard_map/ppermute | solution.py:107
  108.5 1.5 %collective-permute-done.19 = bf16[32,7168]{1,0:T(8,128)(2,1)S(1)} collective-permute-done((bf16[32,7168]{1,0:T(8,128)(2,1)S(1)}, bf16[32,7168]{1,0:T(8,128)(2,1)S(1)}, u32[]{:S(2)}, u32[]{:S(2)}) %collective-permute-start.19) | collective-permute-done | bytes 458784 | tf_op jit(solution)/shard_map/ppermute | solution.py:107
  110.1 0.3 add_convert_fusion.1
  110.4 0.3 collective-permute-start.20
  110.7 3.0 %collective-permute-start.22 = (bf16[32,7168]{1,0:T(8,128)(2,1)S(1)}, bf16[32,7168]{1,0:T(8,128)(2,1)S(1)}, u32[]{:S(2)}, u32[]{:S(2)}) collective-permute-start(bf16[32,7168]{1,0:T(8,128)(2,1)S(1)} %get-tuple-element.61), channel_id=1, source_target_pairs={{0,3},{1,0},{2,1},{3,2},{4,7},{5,4},{6,5},{7,6},{8,11},{9,8},{10,9... | collective-permute-start | bytes 1376264 | tf_op jit(solution)/shard_map/ppermute | solution.py:107
  113.7 8.7 %collective-permute-done.20 = bf16[32,7168]{1,0:T(8,128)(2,1)S(1)} collective-permute-done((bf16[32,7168]{1,0:T(8,128)(2,1)S(1)}, bf16[32,7168]{1,0:T(8,128)(2,1)S(1)}, u32[]{:S(2)}, u32[]{:S(2)}) %collective-permute-start.20) | collective-permute-done | bytes 458784 | tf_op jit(solution)/shard_map/ppermute | solution.py:107
  122.4 0.5 add_convert_fusion
  122.9 1.3 all_to_all.16
  124.2 5.6 %all-to-all-start.1 = ((bf16[32,2,7168]{2,1,0:T(2,128)(2,1)}), bf16[32,2,7168]{2,1,0:T(2,128)(2,1)S(1)}, u32[]{:S(2)}, u32[]{:S(2)}) async-start(bf16[32,2,7168]{2,1,0:T(2,128)(2,1)} %all_to_all.16), calls=%async_computation.1 | async-start | bytes 1835008 | tf_op jit(solution)/shard_map/all_to_all | solution.py:112
  129.9 22.7 %all-to-all-done.1 = bf16[32,2,7168]{2,1,0:T(2,128)(2,1)S(1)} async-done(((bf16[32,2,7168]{2,1,0:T(2,128)(2,1)}), bf16[32,2,7168]{2,1,0:T(2,128)(2,1)S(1)}, u32[]{:S(2)}, u32[]{:S(2)}) %all-to-all-start.1) | async-done | bytes 917536 | tf_op jit(solution)/shard_map/all_to_all | solution.py:112
  152.5 1.2 fusion
  (42 shorter events, 0.9 us)
Async XLA Ops:
  0.0 2.7 %copy-start = (bf16[4,7168]{1,0:T(4,128)(2,1)S(1)}, bf16[4,7168]{1,0:T(4,128)(2,1)}, u32[]{:S(2)}) copy-start(bf16[4,7168]{1,0:T(4,128)(2,1)} %param.6) | copy-start | bytes 172036
  40.5 10.3 %collective-permute-start = (bf16[64,7168]{1,0:T(8,128)(2,1)S(1)}, bf16[64,7168]{1,0:T(8,128)(2,1)S(1)}, u32[]{:S(2)}, u32[]{:S(2)}) collective-permute-start(bf16[64,7168]{1,0:T(8,128)(2,1)S(1)} %all_to_all.15.refs_0_), channel_id=1, source_target_pairs={{0,4},{4,0},{8,12},{12,8},{16,20},{20,16},{24,28},{28,24},{32,36},... | collective-permute-start | bytes 2752520 | tf_op jit(solution)/shard_map/ppermute | solution.py:104
  40.6 24.0 %collective-permute-start.3 = (bf16[64,7168]{1,0:T(8,128)(2,1)S(1)}, bf16[64,7168]{1,0:T(8,128)(2,1)S(1)}, u32[]{:S(2)}, u32[]{:S(2)}) collective-permute-start(bf16[64,7168]{1,0:T(8,128)(2,1)S(1)} %all_to_all.15.refs_0_), channel_id=1, source_target_pairs={{0,1},{1,2},{2,3},{3,0},{4,5},{5,6},{6,7},{7,4},{8,9},{9,10},{10,1... | collective-permute-start | bytes 2752520 | tf_op jit(solution)/shard_map/ppermute | solution.py:107
  42.3 22.4 %collective-permute-start.4 = (bf16[64,7168]{1,0:T(8,128)(2,1)S(1)}, bf16[64,7168]{1,0:T(8,128)(2,1)S(1)}, u32[]{:S(2)}, u32[]{:S(2)}) collective-permute-start(bf16[64,7168]{1,0:T(8,128)(2,1)S(1)} %all_to_all.15.refs_0_), channel_id=1, source_target_pairs={{0,3},{1,0},{2,1},{3,2},{4,7},{5,4},{6,5},{7,6},{8,11},{9,8},{10,9... | collective-permute-start | bytes 2752520 | tf_op jit(solution)/shard_map/ppermute | solution.py:107
  44.0 2.0 %copy-start.1 = (bf16[1,7168,256]{2,1,0:T(8,128)(2,1)S(1)}, bf16[1,7168,256]{2,1,0:T(8,128)(2,1)}, u32[]{:S(2)}) copy-start(bf16[1,7168,256]{2,1,0:T(8,128)(2,1)} %refs_0_.1) | copy-start | bytes 11010052
  46.0 2.0 %copy-start.2 = (bf16[1,7168,256]{2,1,0:T(8,128)(2,1)S(1)}, bf16[1,7168,256]{2,1,0:T(8,128)(2,1)}, u32[]{:S(2)}) copy-start(bf16[1,7168,256]{2,1,0:T(8,128)(2,1)} %refs_1_.1) | copy-start | bytes 11010052
  48.0 2.0 %copy-start.3 = (bf16[1,256,7168]{2,1,0:T(8,128)(2,1)S(1)}, bf16[1,256,7168]{2,1,0:T(8,128)(2,1)}, u32[]{:S(2)}) copy-start(bf16[1,256,7168]{2,1,0:T(8,128)(2,1)} %refs_2_.1) | copy-start | bytes 11010052
  64.7 4.0 %collective-permute-start.5 = (bf16[64,7168]{1,0:T(8,128)(2,1)S(1)}, bf16[64,7168]{1,0:T(8,128)(2,1)S(1)}, u32[]{:S(2)}, u32[]{:S(2)}) collective-permute-start(bf16[64,7168]{1,0:T(8,128)(2,1)S(1)} %get-tuple-element.38.refs_0_), channel_id=1, source_target_pairs={{0,4},{4,0},{8,12},{12,8},{16,20},{20,16},{24,28},{28,24},{32,36},... | collective-permute-start | bytes 2752520 | tf_op jit(solution)/shard_map/ppermute | solution.py:104
  64.7 4.0 %collective-permute-start.6 = (bf16[64,7168]{1,0:T(8,128)(2,1)S(1)}, bf16[64,7168]{1,0:T(8,128)(2,1)S(1)}, u32[]{:S(2)}, u32[]{:S(2)}) collective-permute-start(bf16[64,7168]{1,0:T(8,128)(2,1)S(1)} %get-tuple-element.39.refs_1_), channel_id=1, source_target_pairs={{0,4},{4,0},{8,12},{12,8},{16,20},{20,16},{24,28},{28,24},{32,36},... | collective-permute-start | bytes 2752520 | tf_op jit(solution)/shard_map/ppermute | solution.py:104
  65.2 13.8 %collective-permute-start.11 = (bf16[32,7168]{1,0:T(8,128)(2,1)S(1)}, bf16[32,7168]{1,0:T(8,128)(2,1)S(1)}, u32[]{:S(2)}, u32[]{:S(2)}) collective-permute-start(bf16[32,7168]{1,0:T(8,128)(2,1)S(1)} %slice.25), channel_id=1, source_target_pairs={{0,1},{1,2},{2,3},{3,0},{4,5},{5,6},{6,7},{7,4},{8,9},{9,10},{10,1... | collective-permute-start | bytes 1376264 | tf_op jit(solution)/shard_map/ppermute | solution.py:107
  66.9 12.2 %collective-permute-start.12 = (bf16[32,7168]{1,0:T(8,128)(2,1)S(1)}, bf16[32,7168]{1,0:T(8,128)(2,1)S(1)}, u32[]{:S(2)}, u32[]{:S(2)}) collective-permute-start(bf16[32,7168]{1,0:T(8,128)(2,1)S(1)} %slice.26), channel_id=1, source_target_pairs={{0,3},{1,0},{2,1},{3,2},{4,7},{5,4},{6,5},{7,6},{8,11},{9,8},{10,9... | collective-permute-start | bytes 1376264 | tf_op jit(solution)/shard_map/ppermute | solution.py:107
  71.9 7.7 %collective-permute-start.7 = (bf16[32,7168]{1,0:T(8,128)(2,1)S(1)}, bf16[32,7168]{1,0:T(8,128)(2,1)S(1)}, u32[]{:S(2)}, u32[]{:S(2)}) collective-permute-start(bf16[32,7168]{1,0:T(8,128)(2,1)S(1)} %get-tuple-element.41), channel_id=1, source_target_pairs={{0,4},{4,0},{8,12},{12,8},{16,20},{20,16},{24,28},{28,24},{32,36},... | collective-permute-start | bytes 1376264 | tf_op jit(solution)/shard_map/ppermute | solution.py:104
  72.0 7.6 %collective-permute-start.8 = (bf16[32,7168]{1,0:T(8,128)(2,1)S(1)}, bf16[32,7168]{1,0:T(8,128)(2,1)S(1)}, u32[]{:S(2)}, u32[]{:S(2)}) collective-permute-start(bf16[32,7168]{1,0:T(8,128)(2,1)S(1)} %get-tuple-element.42), channel_id=1, source_target_pairs={{0,4},{4,0},{8,12},{12,8},{16,20},{20,16},{24,28},{28,24},{32,36},... | collective-permute-start | bytes 1376264 | tf_op jit(solution)/shard_map/ppermute | solution.py:104
  72.5 7.1 %collective-permute-start.9 = (bf16[32,7168]{1,0:T(8,128)(2,1)S(1)}, bf16[32,7168]{1,0:T(8,128)(2,1)S(1)}, u32[]{:S(2)}, u32[]{:S(2)}) collective-permute-start(bf16[32,7168]{1,0:T(8,128)(2,1)S(1)} %get-tuple-element.43), channel_id=1, source_target_pairs={{0,4},{4,0},{8,12},{12,8},{16,20},{20,16},{24,28},{28,24},{32,36},... | collective-permute-start | bytes 1376264 | tf_op jit(solution)/shard_map/ppermute | solution.py:104
  79.0 1.8 %collective-permute-start.10 = (bf16[32,7168]{1,0:T(8,128)(2,1)S(1)}, bf16[32,7168]{1,0:T(8,128)(2,1)S(1)}, u32[]{:S(2)}, u32[]{:S(2)}) collective-permute-start(bf16[32,7168]{1,0:T(8,128)(2,1)S(1)} %get-tuple-element.44), channel_id=1, source_target_pairs={{0,4},{4,0},{8,12},{12,8},{16,20},{20,16},{24,28},{28,24},{32,36},... | collective-permute-start | bytes 1376264 | tf_op jit(solution)/shard_map/ppermute | solution.py:104
  79.2 4.1 %collective-permute-start.14 = (bf16[32,7168]{1,0:T(8,128)(2,1)S(1)}, bf16[32,7168]{1,0:T(8,128)(2,1)S(1)}, u32[]{:S(2)}, u32[]{:S(2)}) collective-permute-start(bf16[32,7168]{1,0:T(8,128)(2,1)S(1)} %get-tuple-element.46.refs_5_.refs_1_), channel_id=1, source_target_pairs={{0,4},{4,0},{8,12},{12,8},{16,20},{20,16},{24,28},{28,24},{32,36},... | collective-permute-start | bytes 1376264 | tf_op jit(solution)/shard_map/ppermute | solution.py:104
  80.8 2.5 %collective-permute-start.13 = (bf16[32,7168]{1,0:T(8,128)(2,1)S(1)}, bf16[32,7168]{1,0:T(8,128)(2,1)S(1)}, u32[]{:S(2)}, u32[]{:S(2)}) collective-permute-start(bf16[32,7168]{1,0:T(8,128)(2,1)S(1)} %get-tuple-element.48.refs_0_), channel_id=1, source_target_pairs={{0,4},{4,0},{8,12},{12,8},{16,20},{20,16},{24,28},{28,24},{32,36},... | collective-permute-start | bytes 1376264 | tf_op jit(solution)/shard_map/ppermute | solution.py:104
  81.2 12.9 %collective-permute-start.17 = (bf16[32,7168]{1,0:T(8,128)(2,1)S(1)}, bf16[32,7168]{1,0:T(8,128)(2,1)S(1)}, u32[]{:S(2)}, u32[]{:S(2)}) collective-permute-start(bf16[32,7168]{1,0:T(8,128)(2,1)S(1)} %get-tuple-element.64), channel_id=1, source_target_pairs={{0,3},{1,0},{2,1},{3,2},{4,7},{5,4},{6,5},{7,6},{8,11},{9,8},{10,9... | collective-permute-start | bytes 1376264 | tf_op jit(solution)/shard_map/ppermute | solution.py:107
  83.0 13.6 %collective-permute-start.18 = (bf16[32,7168]{1,0:T(8,128)(2,1)S(1)}, bf16[32,7168]{1,0:T(8,128)(2,1)S(1)}, u32[]{:S(2)}, u32[]{:S(2)}) collective-permute-start(bf16[32,7168]{1,0:T(8,128)(2,1)S(1)} %get-tuple-element.63), channel_id=1, source_target_pairs={{0,1},{1,2},{2,3},{3,0},{4,5},{5,6},{6,7},{7,4},{8,9},{9,10},{10,1... | collective-permute-start | bytes 1376264 | tf_op jit(solution)/shard_map/ppermute | solution.py:107
  85.1 11.6 %collective-permute-start.15 = (bf16[32,7168]{1,0:T(8,128)(2,1)S(1)}, bf16[32,7168]{1,0:T(8,128)(2,1)S(1)}, u32[]{:S(2)}, u32[]{:S(2)}) collective-permute-start(bf16[32,7168]{1,0:T(8,128)(2,1)S(1)} %get-tuple-element.50), channel_id=1, source_target_pairs={{0,4},{4,0},{8,12},{12,8},{16,20},{20,16},{24,28},{28,24},{32,36},... | collective-permute-start | bytes 1376264 | tf_op jit(solution)/shard_map/ppermute | solution.py:104
  85.2 11.5 %collective-permute-start.16 = (bf16[32,7168]{1,0:T(8,128)(2,1)S(1)}, bf16[32,7168]{1,0:T(8,128)(2,1)S(1)}, u32[]{:S(2)}, u32[]{:S(2)}) collective-permute-start(bf16[32,7168]{1,0:T(8,128)(2,1)S(1)} %get-tuple-element.51), channel_id=1, source_target_pairs={{0,4},{4,0},{8,12},{12,8},{16,20},{20,16},{24,28},{28,24},{32,36},... | collective-permute-start | bytes 1376264 | tf_op jit(solution)/shard_map/ppermute | solution.py:104
  96.9 11.7 %collective-permute-start.21 = (bf16[32,7168]{1,0:T(8,128)(2,1)S(1)}, bf16[32,7168]{1,0:T(8,128)(2,1)S(1)}, u32[]{:S(2)}, u32[]{:S(2)}) collective-permute-start(bf16[32,7168]{1,0:T(8,128)(2,1)S(1)} %get-tuple-element.65), channel_id=1, source_target_pairs={{0,3},{1,0},{2,1},{3,2},{4,7},{5,4},{6,5},{7,6},{8,11},{9,8},{10,9... | collective-permute-start | bytes 1376264 | tf_op jit(solution)/shard_map/ppermute | solution.py:107
  97.2 12.8 %collective-permute-start.19 = (bf16[32,7168]{1,0:T(8,128)(2,1)S(1)}, bf16[32,7168]{1,0:T(8,128)(2,1)S(1)}, u32[]{:S(2)}, u32[]{:S(2)}) collective-permute-start(bf16[32,7168]{1,0:T(8,128)(2,1)S(1)} %get-tuple-element.66), channel_id=1, source_target_pairs={{0,1},{1,2},{2,3},{3,0},{4,5},{5,6},{6,7},{7,4},{8,9},{9,10},{10,1... | collective-permute-start | bytes 1376264 | tf_op jit(solution)/shard_map/ppermute | solution.py:107
  99.0 14.8 %collective-permute-start.2 = (bf16[32,7168]{1,0:T(8,128)(2,1)S(1)}, bf16[32,7168]{1,0:T(8,128)(2,1)S(1)}, u32[]{:S(2)}, u32[]{:S(2)}) collective-permute-start(bf16[32,7168]{1,0:T(8,128)(2,1)S(1)} %get-tuple-element.37), channel_id=1, source_target_pairs={{0,4},{4,0},{8,12},{12,8},{16,20},{20,16},{24,28},{28,24},{32,36},... | collective-permute-start | bytes 1376264 | tf_op jit(solution)/shard_map/ppermute | solution.py:104
  99.0 14.8 %collective-permute-start.1 = (bf16[32,7168]{1,0:T(8,128)(2,1)S(1)}, bf16[32,7168]{1,0:T(8,128)(2,1)S(1)}, u32[]{:S(2)}, u32[]{:S(2)}) collective-permute-start(bf16[32,7168]{1,0:T(8,128)(2,1)S(1)} %get-tuple-element.36), channel_id=1, source_target_pairs={{0,4},{4,0},{8,12},{12,8},{16,20},{20,16},{24,28},{28,24},{32,36},... | collective-permute-start | bytes 1376264 | tf_op jit(solution)/shard_map/ppermute | solution.py:104
  110.4 12.0 %collective-permute-start.20 = (bf16[32,7168]{1,0:T(8,128)(2,1)S(1)}, bf16[32,7168]{1,0:T(8,128)(2,1)S(1)}, u32[]{:S(2)}, u32[]{:S(2)}) collective-permute-start(bf16[32,7168]{1,0:T(8,128)(2,1)S(1)} %get-tuple-element.62), channel_id=1, source_target_pairs={{0,1},{1,2},{2,3},{3,0},{4,5},{5,6},{6,7},{7,4},{8,9},{9,10},{10,1... | collective-permute-start | bytes 1376264 | tf_op jit(solution)/shard_map/ppermute | solution.py:107
  110.7 11.7 %collective-permute-start.22 = (bf16[32,7168]{1,0:T(8,128)(2,1)S(1)}, bf16[32,7168]{1,0:T(8,128)(2,1)S(1)}, u32[]{:S(2)}, u32[]{:S(2)}) collective-permute-start(bf16[32,7168]{1,0:T(8,128)(2,1)S(1)} %get-tuple-element.61), channel_id=1, source_target_pairs={{0,3},{1,0},{2,1},{3,2},{4,7},{5,4},{6,5},{7,6},{8,11},{9,8},{10,9... | collective-permute-start | bytes 1376264 | tf_op jit(solution)/shard_map/ppermute | solution.py:107
  124.2 28.4 %all-to-all-start.1 = ((bf16[32,2,7168]{2,1,0:T(2,128)(2,1)}), bf16[32,2,7168]{2,1,0:T(2,128)(2,1)S(1)}, u32[]{:S(2)}, u32[]{:S(2)}) async-start(bf16[32,2,7168]{2,1,0:T(2,128)(2,1)} %all_to_all.16), calls=%async_computation.1 | async-start | bytes 1835008 | tf_op jit(solution)/shard_map/all_to_all | solution.py:112

commit v2 on v1

--- a/solution.py
+++ b/solution.py
@@ -22,7 +22,7 @@
         out_shape=[jax.ShapeDtypeStruct(value.shape, value.dtype) for value in values],
         input_output_aliases={place: place for place in range(len(values))},
         compiler_params=pltpu.CompilerParams(vmem_limit_bytes=MIB),
-        cost_estimate=pl.CostEstimate(flops=0, bytes_accessed=cost, transcendentals=0),
+        cost_estimate=pl.CostEstimate(flops=cost * 64, bytes_accessed=cost, transcendentals=0),
     )(*values, *first)
 
 
@@ -49,9 +49,9 @@
     )(*weights)
 
 
-def ffn_kernel(pieces, tiles, *refs):
-    own_refs, refs = refs[:pieces], refs[pieces:]
-    other_refs, refs = refs[:pieces], refs[pieces:]
+def ffn_kernel(own_count, other_count, tiles, *refs):
+    own_refs, refs = refs[:own_count], refs[own_count:]
+    other_refs, refs = refs[:other_count], refs[other_count:]
     gate_ref, up_ref, down_ref, keep_ref, *send_refs = refs
     half, width = keep_ref.shape
     part = half // len(send_refs)
@@ -75,17 +75,13 @@
     units = gate_weight.shape[2]
     parts = half // PART
     return pl.pallas_call(
-        functools.partial(ffn_kernel, len(own), 4),
-        in_specs=[ONCHIP] * (2 * len(own) + 3),
+        functools.partial(ffn_kernel, len(own), len(other), 4),
+        in_specs=[ONCHIP] * (len(own) + len(other) + 3),
         out_specs=[ONCHIP] * (1 + parts),
         out_shape=[jax.ShapeDtypeStruct((half, width), jnp.bfloat16)]
         + [jax.ShapeDtypeStruct((PART, width), jnp.bfloat16)] * parts,
         compiler_params=pltpu.CompilerParams(vmem_limit_bytes=16 * MIB),
-        cost_estimate=pl.CostEstimate(
-            flops=2 * 2 * half * 3 * width * units,
-            bytes_accessed=3 * width * units * 2 + half * width * 8,
-            transcendentals=2 * half * units,
-        ),
+        cost_estimate=pl.CostEstimate(flops=0, bytes_accessed=0, transcendentals=0),
     )(*own, *other, gate_weight, up_weight, down_weight)
 
 
@@ -119,18 +115,15 @@
     def narrow(value):
         return value.astype(jnp.bfloat16)
 
-    weights = 2.5 * affinity / jnp.sum(affinity, axis=1, keepdims=True)
     labels = jnp.arange(experts, dtype=jnp.int32)
     matches = (expert_ids[:, :, None] == labels[None, None, :]).astype(jnp.float32)
     chosen = jnp.sum(matches, axis=1)
-    shares = jnp.sum(matches * weights[:, :, None], axis=1)
     earlier = jnp.cumsum(chosen, axis=0) - chosen
     slot_values = jnp.arange(slots, dtype=jnp.float32)
     picked = chosen.T[:, None, :] * (earlier.T[:, None, :] == slot_values[None, :, None]).astype(
         jnp.float32
     )
     picked = picked.reshape(count, tok_count)
-    coefficients = picked * jnp.repeat(shares.T, slots, axis=0)
     outgoing = narrow(
         jnp.dot(picked.astype(jnp.bfloat16), tokens, preferred_element_type=jnp.float32)
     )
@@ -138,13 +131,16 @@
     staged = stage(gate_weight, up_weight, down_weight)
 
     own = exchange(outgoing)
-    left, right = over_y(own, 1), over_y(own, -1)
-    own_kept, *own_sent = ffn([own], [over_core(own)], *staged)
-    left, right = after([left, right], own_kept)
+    low, high = own[:half], own[half:]
+    others = [over_core(low), over_core(high)]
+    near = [over_y(low, 1), over_y(high, -1)]
+    own_kept, *own_sent = ffn([low, high], others, *staged)
+    near = [*after(near, own_kept), over_y(high, 1), over_y(low, -1)]
 
-    far = [over_y(left[:half], 1), over_y(right[half:], -1)]
-    near = [left, right]
-    near_kept, *near_sent = ffn(near, [over_core(piece) for piece in near], *staged)
+    far = [over_y(near[0], 1), over_y(near[1], -1)]
+    quarter = half // 2
+    traded = [over_core(part) for piece in near for part in (piece[:quarter], piece[quarter:])]
+    near_kept, *near_sent = ffn(near, traded, *staged)
     far = after(far, near_kept, cost=WAIT)
     *near_got, far_low = after([*map(over_core, near_sent), far[0]], far[1])
     far = [far_low, far[1]]
@@ -153,20 +149,24 @@
         for place, got in enumerate(near_got)
     ]
 
-    to_left, to_right = over_y(narrow(near_sum[0]), -1), over_y(narrow(near_sum[3]), 1)
+    to_left, to_right = over_y(narrow(near_sum[0]), -1), over_y(narrow(near_sum[1]), 1)
     far_kept, *far_sent = ffn(far, [over_core(piece) for piece in far], *staged)
     to_left, to_right = after([to_left, to_right], far_kept, cost=WAIT)
     far_got = after([*map(over_core, far_sent)], to_left, to_right)
 
     passed_right = over_y(narrow(wide(far_kept[:half]) + wide(far_got[0])), 1)
     passed_left = over_y(narrow(wide(far_kept[half:]) + wide(far_got[1])), -1)
-    last_right = over_y(narrow(near_sum[2] + wide(passed_right)), 1)
-    last_left = over_y(narrow(near_sum[1] + wide(passed_left)), -1)
+    last_right = over_y(narrow(near_sum[3] + wide(passed_right)), 1)
+    last_left = over_y(narrow(near_sum[2] + wide(passed_left)), -1)
     own_got = jnp.concatenate([over_core(piece) for piece in own_sent], axis=0)
     from_left = wide(jnp.concatenate([last_right, to_right], axis=0))
     from_right = wide(jnp.concatenate([to_left, last_left], axis=0))
     own_total = wide(own_kept) + wide(own_got)
     returned = exchange(narrow(own_total + from_left + from_right))
+    (affinity,) = after([affinity], own_kept)
+    weights = 2.5 * affinity / jnp.sum(affinity, axis=1, keepdims=True)
+    shares = jnp.sum(matches * weights[:, :, None], axis=1)
+    coefficients = picked * jnp.repeat(shares.T, slots, axis=0)
     mixed = jnp.dot(
         coefficients.T,
         wide(returned),

time: 154 us -> 152 us (0.987)
  waiting for transfers between devices: 72.8 us -> 64.4 us
  starting transfers between devices: 22.7 us -> 28.6 us
    ppermute x10 -> x12, waiting for transfers between devices: 48.8 us -> 37 us  [over_y(): lax.ppermute(value, 'tp', [(i, (i + shift) % tp_count) for i in range(tp_...]
    ppermute x10 -> x12, starting transfers between devices: 14.2 us -> 17.9 us  [over_y(): lax.ppermute(value, 'tp', [(i, (i + shift) % tp_count) for i in range(tp_...]
    ppermute x13 -> x20, waiting for transfers between devices: 1.32 us -> 4.98 us  [over_core(): return lax.ppermute(value, 'ep', [(i, i ^ 1) for i in range(ep_count)])]
    ppermute x13 -> x20, starting transfers between devices: 2.89 us -> 4.94 us  [over_core(): return lax.ppermute(value, 'ep', [(i, i ^ 1) for i in range(ep_count)])]
    unnamed x8 -> x11, local copies, waits for them, and re-layouts: 6.12 us -> 6.81 us
  transfers between devices with their start and end apart: 24 -> 33, of which waited for: 10 -> 18; matrix products, arithmetic and copies ran while one was open for 0% -> 1% of each run, Pallas kernels for 5% -> 5%
where the time goes in v2:
time: 152 us; the launch traced here: 151 us
  waiting for transfers between devices  64.4 us (42%)
  blocking collectives  36.7 us (24%)
  starting transfers between devices  28.6 us (19%)
  local copies, waits for them, and re-layouts  9.95 us (7%)
  Pallas kernels  7.43 us (5%)
  other arithmetic  2.33 us (2%)
  matrix products  1.61 us (1%)
    ppermute x12, waiting for transfers between devices, over_y(): lax.ppermute(value, 'tp', [(i, (i + shift) % tp_count) for i in range(tp_...  37 us
    all_to_all x1, blocking collectives, exchange(): lax.all_to_all(value, 'ep', split_axis=0, concat_axis=0, axis_index_group...  36.7 us
    all_to_all x1, waiting for transfers between devices, exchange(): lax.all_to_all(value, 'ep', split_axis=0, concat_axis=0, axis_index_group...  22.4 us
    ppermute x12, starting transfers between devices, over_y(): lax.ppermute(value, 'tp', [(i, (i + shift) % tp_count) for i in range(tp_...  17.9 us
    unnamed x11, local copies, waits for them, and re-layouts  6.81 us
    pallas_call x3, Pallas kernels, ffn(): pl.pallas_call(functools.partial(ffn_kernel, len(own), len(other), 4), in...  6.66 us
    all_to_all x1, starting transfers between devices, exchange(): lax.all_to_all(value, 'ep', split_axis=0, concat_axis=0, axis_index_group...  5.75 us
    ppermute x20, waiting for transfers between devices, over_core(): return lax.ppermute(value, 'ep', [(i, i ^ 1) for i in range(ep_count)])  4.98 us
  transfers between devices with their start and end apart: 33, of which 18 were waited for; matrix products, arithmetic and copies ran while one was open for 1% of the time, Pallas kernels for 5%

profile of v2, /device:TPU:2, one launch (start us, length us, event | category | flops | bytes accessed | tf_op | source)
XLA Modules:
  0.0 151.2 jit_solution(17971429058536007280)
XLA Ops:
  0.0 0.7 copy.50.refs_0_
  0.7 0.8 convert_reduce_fusion
  1.9 0.4 convolution_convert_fusion
  2.3 0.3 all_to_all.12
  2.6 36.7 %all_to_all.18 = bf16[32,2,7168]{2,1,0:T(2,128)(2,1)S(1)} all-to-all(bf16[32,2,7168]{2,1,0:T(2,128)(2,1)S(1)} %all_to_all.12), channel_id=1, replica_groups={{0,8,16,24,32,40,48,56,64,72,80,88,96,104,112,120,128,136,144,152,160,1..., dimensions={0} | all-to-all | bytes 1835008 | tf_op jit(solution)/shard_map/all_to_all | solution.py:108
  39.3 0.6 fusion.7
  40.4 0.6 collective-permute-start.1
  41.0 1.6 %collective-permute-start.4 = (bf16[32,7168]{1,0:T(8,128)(2,1)S(1)}, bf16[32,7168]{1,0:T(8,128)(2,1)S(1)}, u32[]{:S(2)}, u32[]{:S(2)}) collective-permute-start(bf16[32,7168]{1,0:T(8,128)(2,1)S(1)} %slice.55.refs_0_), channel_id=1, source_target_pairs={{0,1},{1,2},{2,3},{3,0},{4,5},{5,6},{6,7},{7,4},{8,9},{9,10},{10,1... | collective-permute-start | bytes 1376264 | tf_op jit(solution)/shard_map/ppermute | solution.py:103
  42.6 1.7 %collective-permute-start.5 = (bf16[32,7168]{1,0:T(8,128)(2,1)S(1)}, bf16[32,7168]{1,0:T(8,128)(2,1)S(1)}, u32[]{:S(2)}, u32[]{:S(2)}) collective-permute-start(bf16[32,7168]{1,0:T(8,128)(2,1)S(1)} %slice.57.refs_1_), channel_id=1, source_target_pairs={{0,3},{1,0},{2,1},{3,2},{4,7},{5,4},{6,5},{7,6},{8,11},{9,8},{10,9... | collective-permute-start | bytes 1376264 | tf_op jit(solution)/shard_map/ppermute | solution.py:103
  44.2 2.0 %copy-done.1 = bf16[1,7168,256]{2,1,0:T(8,128)(2,1)S(1)} copy-done((bf16[1,7168,256]{2,1,0:T(8,128)(2,1)S(1)}, bf16[1,7168,256]{2,1,0:T(8,128)(2,1)}, u32[]{:S(2)}) %copy-start.1) | copy-done | bytes 3670040
  46.3 2.0 %copy-done.2 = bf16[1,7168,256]{2,1,0:T(8,128)(2,1)S(1)} copy-done((bf16[1,7168,256]{2,1,0:T(8,128)(2,1)S(1)}, bf16[1,7168,256]{2,1,0:T(8,128)(2,1)}, u32[]{:S(2)}) %copy-start.2) | copy-done | bytes 3670040
  48.3 2.0 %copy-done.3 = bf16[1,256,7168]{2,1,0:T(8,128)(2,1)S(1)} copy-done((bf16[1,256,7168]{2,1,0:T(8,128)(2,1)S(1)}, bf16[1,256,7168]{2,1,0:T(8,128)(2,1)}, u32[]{:S(2)}) %copy-start.3) | copy-done | bytes 3670040
  50.3 0.8 shard_map.64
  51.1 0.4 collective-permute-start.6
  51.6 2.9 %collective-permute-start.7 = (bf16[32,7168]{1,0:T(8,128)(2,1)S(1)}, bf16[32,7168]{1,0:T(8,128)(2,1)S(1)}, u32[]{:S(2)}, u32[]{:S(2)}) collective-permute-start(bf16[32,7168]{1,0:T(8,128)(2,1)S(1)} %slice.55.refs_0_), channel_id=1, source_target_pairs={{0,3},{1,0},{2,1},{3,2},{4,7},{5,4},{6,5},{7,6},{8,11},{9,8},{10,9... | collective-permute-start | bytes 1376264 | tf_op jit(solution)/shard_map/ppermute | solution.py:103
  54.4 1.8 %shard_map.65 = (bf16[64,7168]{1,0:T(8,128)(2,1)S(1)}, bf16[32,7168]{1,0:T(8,128)(2,1)S(1)}, bf16[32,7168]{1,0:T(8,128)(2,1)S(1)}) custom-call(bf16[32,7168]{1,0:T(8,128)(2,1)S(1)} %slice.55.refs_0_, bf16[32,7168]{1,0:T(8,128)(2,1)S(1)} %slice.57.refs_1_, bf16[32,7168]{1,0:T(8,128)(2,1)S(1)} %collective-permute-done.refs_2_, ...), custom_call_target="tpu_custom_call" | custom-call | tf_op jit(solution)/shard_map/pallas_call | solution.py:77
  56.3 1.4 collective-permute-start.20
  57.7 2.0 %collective-permute-start.21 = (bf16[32,7168]{1,0:T(8,128)(2,1)S(1)}, bf16[32,7168]{1,0:T(8,128)(2,1)S(1)}, u32[]{:S(2)}, u32[]{:S(2)}) collective-permute-start(bf16[32,7168]{1,0:T(8,128)(2,1)S(1)} %get-tuple-element.39.refs_1_), channel_id=1, source_target_pairs={{0,3},{1,0},{2,1},{3,2},{4,7},{5,4},{6,5},{7,6},{8,11},{9,8},{10,9... | collective-permute-start | bytes 1376264 | tf_op jit(solution)/shard_map/ppermute | solution.py:103
  59.7 6.1 %collective-permute-done.6.refs_2_ = bf16[32,7168]{1,0:T(8,128)(2,1)S(1)} collective-permute-done((bf16[32,7168]{1,0:T(8,128)(2,1)S(1)}, bf16[32,7168]{1,0:T(8,128)(2,1)S(1)}, u32[]{:S(2)}, u32[]{:S(2)}) %collective-permute-start.6) | collective-permute-done | bytes 458784 | tf_op jit(solution)/shard_map/ppermute | solution.py:103
  65.9 0.6 collective-permute-start.10
  66.8 0.6 collective-permute-done.9.refs_5_
  68.3 0.5 collective-permute-done.12.refs_8_
  69.5 0.8 collective-permute-done.15.refs_11_
  70.3 3.1 %shard_map.68 = (bf16[128,7168]{1,0:T(8,128)(2,1)S(1)}, bf16[32,7168]{1,0:T(8,128)(2,1)S(1)}, bf16[32,7168]{1,0:T(8,128)(2,1)S(1)}, bf16[32,7168]{1,0:T(8,128)(2,1)S(1)}, bf16[32,7168]{1,0:T(8,128)(2,1)S(1)}) custom-call(bf16[32,7168]{1,0:T(8,128)(2,1)S(1)} %get-tuple-element.38.refs_0_, bf16[32,7168]{1,0:T(8,128)(2,1)S(1)} %get-tuple-element.39.refs_1_, ...), custom_call_target="tpu_custom_call" | custom-call | tf_op jit(solution)/shard_map/pallas_call | solution.py:77
  73.7 0.4 collective-permute-start.17
  74.6 0.4 collective-permute-start.23
  75.0 0.4 collective-permute-done.16.refs_0_
  75.4 0.7 collective-permute-done.17.refs_1_
  76.0 0.7 collective-permute-done.18.refs_2_
  76.7 0.7 collective-permute-done.19.refs_3_
  77.7 2.6 %collective-permute-start.26 = (bf16[32,7168]{1,0:T(8,128)(2,1)S(1)}, bf16[32,7168]{1,0:T(8,128)(2,1)S(1)}, u32[]{:S(2)}, u32[]{:S(2)}) collective-permute-start(bf16[32,7168]{1,0:T(8,128)(2,1)S(1)} %get-tuple-element.62), channel_id=1, source_target_pairs={{0,3},{1,0},{2,1},{3,2},{4,7},{5,4},{6,5},{7,6},{8,11},{9,8},{10,9... | collective-permute-start | bytes 1376264 | tf_op jit(solution)/shard_map/ppermute | solution.py:103
  80.2 1.7 %shard_map.71 = (bf16[64,7168]{1,0:T(8,128)(2,1)S(1)}, bf16[32,7168]{1,0:T(8,128)(2,1)S(1)}, bf16[32,7168]{1,0:T(8,128)(2,1)S(1)}) custom-call(bf16[32,7168]{1,0:T(8,128)(2,1)S(1)} %get-tuple-element.48.refs_0_, bf16[32,7168]{1,0:T(8,128)(2,1)S(1)} %get-tuple-element.46.refs_5_.refs_1_, bf16[32,7168]{1,0:T(8,128)(2,1)S(1)} %collective-permute-done.22.refs_2_, ...), custom_call_target="tpu_custom_call" | custom-call | tf_op jit(solution)/shard_map/pallas_call | solution.py:77
  82.1 0.5 collective-permute-start.25
  82.6 8.0 %collective-permute-done.26.refs_0_ = bf16[32,7168]{1,0:T(8,128)(2,1)S(1)} collective-permute-done((bf16[32,7168]{1,0:T(8,128)(2,1)S(1)}, bf16[32,7168]{1,0:T(8,128)(2,1)S(1)}, u32[]{:S(2)}, u32[]{:S(2)}) %collective-permute-start.26) | collective-permute-done | bytes 458784 | tf_op jit(solution)/shard_map/ppermute | solution.py:103
  90.6 3.4 %collective-permute-done.27.refs_1_ = bf16[32,7168]{1,0:T(8,128)(2,1)S(1)} collective-permute-done((bf16[32,7168]{1,0:T(8,128)(2,1)S(1)}, bf16[32,7168]{1,0:T(8,128)(2,1)S(1)}, u32[]{:S(2)}, u32[]{:S(2)}) %collective-permute-start.27) | collective-permute-done | bytes 458784 | tf_op jit(solution)/shard_map/ppermute | solution.py:103
  94.1 0.4 collective-permute-start.30
  94.5 1.7 %collective-permute-start.28 = (bf16[32,7168]{1,0:T(8,128)(2,1)S(1)}, bf16[32,7168]{1,0:T(8,128)(2,1)S(1)}, u32[]{:S(2)}, u32[]{:S(2)}) collective-permute-start(bf16[32,7168]{1,0:T(8,128)(2,1)S(1)} %get-tuple-element.64), channel_id=1, source_target_pairs={{0,1},{1,2},{2,3},{3,0},{4,5},{5,6},{6,7},{7,4},{8,9},{9,10},{10,1... | collective-permute-start | bytes 1376264 | tf_op jit(solution)/shard_map/ppermute | solution.py:103
  96.2 0.5 collective-permute-start.2
  96.8 9.1 %collective-permute-done.30 = bf16[32,7168]{1,0:T(8,128)(2,1)S(1)} collective-permute-done((bf16[32,7168]{1,0:T(8,128)(2,1)S(1)}, bf16[32,7168]{1,0:T(8,128)(2,1)S(1)}, u32[]{:S(2)}, u32[]{:S(2)}) %collective-permute-start.30) | collective-permute-done | bytes 458784 | tf_op jit(solution)/shard_map/ppermute | solution.py:103
  105.8 1.5 %collective-permute-done.28 = bf16[32,7168]{1,0:T(8,128)(2,1)S(1)} collective-permute-done((bf16[32,7168]{1,0:T(8,128)(2,1)S(1)}, bf16[32,7168]{1,0:T(8,128)(2,1)S(1)}, u32[]{:S(2)}, u32[]{:S(2)}) %collective-permute-start.28) | collective-permute-done | bytes 458784 | tf_op jit(solution)/shard_map/ppermute | solution.py:103
  107.4 0.3 add_convert_fusion.1
  108.0 3.0 %collective-permute-start.31 = (bf16[32,7168]{1,0:T(8,128)(2,1)S(1)}, bf16[32,7168]{1,0:T(8,128)(2,1)S(1)}, u32[]{:S(2)}, u32[]{:S(2)}) collective-permute-start(bf16[32,7168]{1,0:T(8,128)(2,1)S(1)} %get-tuple-element.59), channel_id=1, source_target_pairs={{0,3},{1,0},{2,1},{3,2},{4,7},{5,4},{6,5},{7,6},{8,11},{9,8},{10,9... | collective-permute-start | bytes 1376264 | tf_op jit(solution)/shard_map/ppermute | solution.py:103
  111.0 8.7 %collective-permute-done.29 = bf16[32,7168]{1,0:T(8,128)(2,1)S(1)} collective-permute-done((bf16[32,7168]{1,0:T(8,128)(2,1)S(1)}, bf16[32,7168]{1,0:T(8,128)(2,1)S(1)}, u32[]{:S(2)}, u32[]{:S(2)}) %collective-permute-start.29) | collective-permute-done | bytes 458784 | tf_op jit(solution)/shard_map/ppermute | solution.py:103
  119.7 0.5 add_convert_fusion
  120.2 1.3 all_to_all.14
  121.5 5.8 %all-to-all-start.1 = ((bf16[32,2,7168]{2,1,0:T(2,128)(2,1)}), bf16[32,2,7168]{2,1,0:T(2,128)(2,1)S(1)}, u32[]{:S(2)}, u32[]{:S(2)}) async-start(bf16[32,2,7168]{2,1,0:T(2,128)(2,1)} %all_to_all.14), calls=%async_computation.1 | async-start | bytes 1835008 | tf_op jit(solution)/shard_map/all_to_all | solution.py:108
  127.7 22.4 %all-to-all-done.1 = bf16[32,2,7168]{2,1,0:T(2,128)(2,1)S(1)} async-done(((bf16[32,2,7168]{2,1,0:T(2,128)(2,1)}), bf16[32,2,7168]{2,1,0:T(2,128)(2,1)S(1)}, u32[]{:S(2)}, u32[]{:S(2)}) %all-to-all-start.1) | async-done | bytes 917536 | tf_op jit(solution)/shard_map/all_to_all | solution.py:108
  150.1 1.2 fusion
  (69 shorter events, 5.0 us)
Async XLA Ops:
  0.0 1.8 %copy-start = (bf16[4,7168]{1,0:T(4,128)(2,1)S(1)}, bf16[4,7168]{1,0:T(4,128)(2,1)}, u32[]{:S(2)}) copy-start(bf16[4,7168]{1,0:T(4,128)(2,1)} %param.6) | copy-start | bytes 172036
  40.1 11.4 %collective-permute-start = (bf16[32,7168]{1,0:T(8,128)(2,1)S(1)}, bf16[32,7168]{1,0:T(8,128)(2,1)S(1)}, u32[]{:S(2)}, u32[]{:S(2)}) collective-permute-start(bf16[32,7168]{1,0:T(8,128)(2,1)S(1)} %slice.55.refs_0_), channel_id=1, source_target_pairs={{0,4},{4,0},{8,12},{12,8},{16,20},{20,16},{24,28},{28,24},{32,36},... | collective-permute-start | bytes 1376264 | tf_op jit(solution)/shard_map/ppermute | solution.py:100
  40.4 14.0 %collective-permute-start.1 = (bf16[32,7168]{1,0:T(8,128)(2,1)S(1)}, bf16[32,7168]{1,0:T(8,128)(2,1)S(1)}, u32[]{:S(2)}, u32[]{:S(2)}) collective-permute-start(bf16[32,7168]{1,0:T(8,128)(2,1)S(1)} %slice.57.refs_1_), channel_id=1, source_target_pairs={{0,4},{4,0},{8,12},{12,8},{16,20},{20,16},{24,28},{28,24},{32,36},... | collective-permute-start | bytes 1376264 | tf_op jit(solution)/shard_map/ppermute | solution.py:100
  41.0 15.2 %collective-permute-start.4 = (bf16[32,7168]{1,0:T(8,128)(2,1)S(1)}, bf16[32,7168]{1,0:T(8,128)(2,1)S(1)}, u32[]{:S(2)}, u32[]{:S(2)}) collective-permute-start(bf16[32,7168]{1,0:T(8,128)(2,1)S(1)} %slice.55.refs_0_), channel_id=1, source_target_pairs={{0,1},{1,2},{2,3},{3,0},{4,5},{5,6},{6,7},{7,4},{8,9},{9,10},{10,1... | collective-permute-start | bytes 1376264 | tf_op jit(solution)/shard_map/ppermute | solution.py:103
  42.6 13.7 %collective-permute-start.5 = (bf16[32,7168]{1,0:T(8,128)(2,1)S(1)}, bf16[32,7168]{1,0:T(8,128)(2,1)S(1)}, u32[]{:S(2)}, u32[]{:S(2)}) collective-permute-start(bf16[32,7168]{1,0:T(8,128)(2,1)S(1)} %slice.57.refs_1_), channel_id=1, source_target_pairs={{0,3},{1,0},{2,1},{3,2},{4,7},{5,4},{6,5},{7,6},{8,11},{9,8},{10,9... | collective-permute-start | bytes 1376264 | tf_op jit(solution)/shard_map/ppermute | solution.py:103
  44.2 2.0 %copy-start.1 = (bf16[1,7168,256]{2,1,0:T(8,128)(2,1)S(1)}, bf16[1,7168,256]{2,1,0:T(8,128)(2,1)}, u32[]{:S(2)}) copy-start(bf16[1,7168,256]{2,1,0:T(8,128)(2,1)} %refs_0_.2) | copy-start | bytes 11010052
  46.3 2.0 %copy-start.2 = (bf16[1,7168,256]{2,1,0:T(8,128)(2,1)S(1)}, bf16[1,7168,256]{2,1,0:T(8,128)(2,1)}, u32[]{:S(2)}) copy-start(bf16[1,7168,256]{2,1,0:T(8,128)(2,1)} %refs_1_.1) | copy-start | bytes 11010052
  48.3 2.0 %copy-start.3 = (bf16[1,256,7168]{2,1,0:T(8,128)(2,1)S(1)}, bf16[1,256,7168]{2,1,0:T(8,128)(2,1)}, u32[]{:S(2)}) copy-start(bf16[1,256,7168]{2,1,0:T(8,128)(2,1)} %refs_2_.1) | copy-start | bytes 11010052
  51.1 14.7 %collective-permute-start.6 = (bf16[32,7168]{1,0:T(8,128)(2,1)S(1)}, bf16[32,7168]{1,0:T(8,128)(2,1)S(1)}, u32[]{:S(2)}, u32[]{:S(2)}) collective-permute-start(bf16[32,7168]{1,0:T(8,128)(2,1)S(1)} %slice.57.refs_1_), channel_id=1, source_target_pairs={{0,1},{1,2},{2,3},{3,0},{4,5},{5,6},{6,7},{7,4},{8,9},{9,10},{10,1... | collective-permute-start | bytes 1376264 | tf_op jit(solution)/shard_map/ppermute | solution.py:103
  51.6 14.3 %collective-permute-start.7 = (bf16[32,7168]{1,0:T(8,128)(2,1)S(1)}, bf16[32,7168]{1,0:T(8,128)(2,1)S(1)}, u32[]{:S(2)}, u32[]{:S(2)}) collective-permute-start(bf16[32,7168]{1,0:T(8,128)(2,1)S(1)} %slice.55.refs_0_), channel_id=1, source_target_pairs={{0,3},{1,0},{2,1},{3,2},{4,7},{5,4},{6,5},{7,6},{8,11},{9,8},{10,9... | collective-permute-start | bytes 1376264 | tf_op jit(solution)/shard_map/ppermute | solution.py:103
  56.3 18.1 %collective-permute-start.20 = (bf16[32,7168]{1,0:T(8,128)(2,1)S(1)}, bf16[32,7168]{1,0:T(8,128)(2,1)S(1)}, u32[]{:S(2)}, u32[]{:S(2)}) collective-permute-start(bf16[32,7168]{1,0:T(8,128)(2,1)S(1)} %get-tuple-element.38.refs_0_), channel_id=1, source_target_pairs={{0,1},{1,2},{2,3},{3,0},{4,5},{5,6},{6,7},{7,4},{8,9},{9,10},{10,1... | collective-permute-start | bytes 1376264 | tf_op jit(solution)/shard_map/ppermute | solution.py:103
  57.7 16.9 %collective-permute-start.21 = (bf16[32,7168]{1,0:T(8,128)(2,1)S(1)}, bf16[32,7168]{1,0:T(8,128)(2,1)S(1)}, u32[]{:S(2)}, u32[]{:S(2)}) collective-permute-start(bf16[32,7168]{1,0:T(8,128)(2,1)S(1)} %get-tuple-element.39.refs_1_), channel_id=1, source_target_pairs={{0,3},{1,0},{2,1},{3,2},{4,7},{5,4},{6,5},{7,6},{8,11},{9,8},{10,9... | collective-permute-start | bytes 1376264 | tf_op jit(solution)/shard_map/ppermute | solution.py:103
  59.7 6.8 %collective-permute-start.8 = (bf16[16,7168]{1,0:T(8,128)(2,1)S(1)}, bf16[16,7168]{1,0:T(8,128)(2,1)S(1)}, u32[]{:S(2)}, u32[]{:S(2)}) collective-permute-start(bf16[16,7168]{1,0:T(8,128)(2,1)S(1)} %get-tuple-element.74), channel_id=1, source_target_pairs={{0,4},{4,0},{8,12},{12,8},{16,20},{20,16},{24,28},{28,24},{32,36},... | collective-permute-start | bytes 688136 | tf_op jit(solution)/shard_map/ppermute | solution.py:100
  65.8 1.5 collective-permute-start.9
  65.9 1.8 %collective-permute-start.10 = (bf16[16,7168]{1,0:T(8,128)(2,1)S(1)}, bf16[16,7168]{1,0:T(8,128)(2,1)S(1)}, u32[]{:S(2)}, u32[]{:S(2)}) collective-permute-start(bf16[16,7168]{1,0:T(8,128)(2,1)S(1)} %get-tuple-element.72), channel_id=1, source_target_pairs={{0,4},{4,0},{8,12},{12,8},{16,20},{20,16},{24,28},{28,24},{32,36},... | collective-permute-start | bytes 688136 | tf_op jit(solution)/shard_map/ppermute | solution.py:100
  66.5 1.5 collective-permute-start.11
  67.3 1.5 collective-permute-start.12
  67.7 1.5 collective-permute-start.13
  68.0 1.5 collective-permute-start.14
  68.8 1.5 collective-permute-start.15
  73.5 1.9 %collective-permute-start.16 = (bf16[32,7168]{1,0:T(8,128)(2,1)S(1)}, bf16[32,7168]{1,0:T(8,128)(2,1)S(1)}, u32[]{:S(2)}, u32[]{:S(2)}) collective-permute-start(bf16[32,7168]{1,0:T(8,128)(2,1)S(1)} %get-tuple-element.41), channel_id=1, source_target_pairs={{0,4},{4,0},{8,12},{12,8},{16,20},{20,16},{24,28},{28,24},{32,36},... | collective-permute-start | bytes 1376264 | tf_op jit(solution)/shard_map/ppermute | solution.py:100
  73.7 2.3 %collective-permute-start.17 = (bf16[32,7168]{1,0:T(8,128)(2,1)S(1)}, bf16[32,7168]{1,0:T(8,128)(2,1)S(1)}, u32[]{:S(2)}, u32[]{:S(2)}) collective-permute-start(bf16[32,7168]{1,0:T(8,128)(2,1)S(1)} %get-tuple-element.42), channel_id=1, source_target_pairs={{0,4},{4,0},{8,12},{12,8},{16,20},{20,16},{24,28},{28,24},{32,36},... | collective-permute-start | bytes 1376264 | tf_op jit(solution)/shard_map/ppermute | solution.py:100
  74.1 2.6 %collective-permute-start.18 = (bf16[32,7168]{1,0:T(8,128)(2,1)S(1)}, bf16[32,7168]{1,0:T(8,128)(2,1)S(1)}, u32[]{:S(2)}, u32[]{:S(2)}) collective-permute-start(bf16[32,7168]{1,0:T(8,128)(2,1)S(1)} %get-tuple-element.43), channel_id=1, source_target_pairs={{0,4},{4,0},{8,12},{12,8},{16,20},{20,16},{24,28},{28,24},{32,36},... | collective-permute-start | bytes 1376264 | tf_op jit(solution)/shard_map/ppermute | solution.py:100
  74.4 2.9 %collective-permute-start.19 = (bf16[32,7168]{1,0:T(8,128)(2,1)S(1)}, bf16[32,7168]{1,0:T(8,128)(2,1)S(1)}, u32[]{:S(2)}, u32[]{:S(2)}) collective-permute-start(bf16[32,7168]{1,0:T(8,128)(2,1)S(1)} %get-tuple-element.44), channel_id=1, source_target_pairs={{0,4},{4,0},{8,12},{12,8},{16,20},{20,16},{24,28},{28,24},{32,36},... | collective-permute-start | bytes 1376264 | tf_op jit(solution)/shard_map/ppermute | solution.py:100
  74.6 5.7 %collective-permute-start.23 = (bf16[32,7168]{1,0:T(8,128)(2,1)S(1)}, bf16[32,7168]{1,0:T(8,128)(2,1)S(1)}, u32[]{:S(2)}, u32[]{:S(2)}) collective-permute-start(bf16[32,7168]{1,0:T(8,128)(2,1)S(1)} %get-tuple-element.46.refs_5_.refs_1_), channel_id=1, source_target_pairs={{0,4},{4,0},{8,12},{12,8},{16,20},{20,16},{24,28},{28,24},{32,36},... | collective-permute-start | bytes 1376264 | tf_op jit(solution)/shard_map/ppermute | solution.py:100
  77.3 2.9 %collective-permute-start.22 = (bf16[32,7168]{1,0:T(8,128)(2,1)S(1)}, bf16[32,7168]{1,0:T(8,128)(2,1)S(1)}, u32[]{:S(2)}, u32[]{:S(2)}) collective-permute-start(bf16[32,7168]{1,0:T(8,128)(2,1)S(1)} %get-tuple-element.48.refs_0_), channel_id=1, source_target_pairs={{0,4},{4,0},{8,12},{12,8},{16,20},{20,16},{24,28},{28,24},{32,36},... | collective-permute-start | bytes 1376264 | tf_op jit(solution)/shard_map/ppermute | solution.py:100
  77.7 12.9 %collective-permute-start.26 = (bf16[32,7168]{1,0:T(8,128)(2,1)S(1)}, bf16[32,7168]{1,0:T(8,128)(2,1)S(1)}, u32[]{:S(2)}, u32[]{:S(2)}) collective-permute-start(bf16[32,7168]{1,0:T(8,128)(2,1)S(1)} %get-tuple-element.62), channel_id=1, source_target_pairs={{0,3},{1,0},{2,1},{3,2},{4,7},{5,4},{6,5},{7,6},{8,11},{9,8},{10,9... | collective-permute-start | bytes 1376264 | tf_op jit(solution)/shard_map/ppermute | solution.py:103
  80.2 13.7 %collective-permute-start.27 = (bf16[32,7168]{1,0:T(8,128)(2,1)S(1)}, bf16[32,7168]{1,0:T(8,128)(2,1)S(1)}, u32[]{:S(2)}, u32[]{:S(2)}) collective-permute-start(bf16[32,7168]{1,0:T(8,128)(2,1)S(1)} %get-tuple-element.61), channel_id=1, source_target_pairs={{0,1},{1,2},{2,3},{3,0},{4,5},{5,6},{6,7},{7,4},{8,9},{9,10},{10,1... | collective-permute-start | bytes 1376264 | tf_op jit(solution)/shard_map/ppermute | solution.py:103
  82.0 11.9 %collective-permute-start.24 = (bf16[32,7168]{1,0:T(8,128)(2,1)S(1)}, bf16[32,7168]{1,0:T(8,128)(2,1)S(1)}, u32[]{:S(2)}, u32[]{:S(2)}) collective-permute-start(bf16[32,7168]{1,0:T(8,128)(2,1)S(1)} %get-tuple-element.50), channel_id=1, source_target_pairs={{0,4},{4,0},{8,12},{12,8},{16,20},{20,16},{24,28},{28,24},{32,36},... | collective-permute-start | bytes 1376264 | tf_op jit(solution)/shard_map/ppermute | solution.py:100
  82.1 11.8 %collective-permute-start.25 = (bf16[32,7168]{1,0:T(8,128)(2,1)S(1)}, bf16[32,7168]{1,0:T(8,128)(2,1)S(1)}, u32[]{:S(2)}, u32[]{:S(2)}) collective-permute-start(bf16[32,7168]{1,0:T(8,128)(2,1)S(1)} %get-tuple-element.51), channel_id=1, source_target_pairs={{0,4},{4,0},{8,12},{12,8},{16,20},{20,16},{24,28},{28,24},{32,36},... | collective-permute-start | bytes 1376264 | tf_op jit(solution)/shard_map/ppermute | solution.py:100
  94.1 11.7 %collective-permute-start.30 = (bf16[32,7168]{1,0:T(8,128)(2,1)S(1)}, bf16[32,7168]{1,0:T(8,128)(2,1)S(1)}, u32[]{:S(2)}, u32[]{:S(2)}) collective-permute-start(bf16[32,7168]{1,0:T(8,128)(2,1)S(1)} %get-tuple-element.63), channel_id=1, source_target_pairs={{0,3},{1,0},{2,1},{3,2},{4,7},{5,4},{6,5},{7,6},{8,11},{9,8},{10,9... | collective-permute-start | bytes 1376264 | tf_op jit(solution)/shard_map/ppermute | solution.py:103
  94.5 12.9 %collective-permute-start.28 = (bf16[32,7168]{1,0:T(8,128)(2,1)S(1)}, bf16[32,7168]{1,0:T(8,128)(2,1)S(1)}, u32[]{:S(2)}, u32[]{:S(2)}) collective-permute-start(bf16[32,7168]{1,0:T(8,128)(2,1)S(1)} %get-tuple-element.64), channel_id=1, source_target_pairs={{0,1},{1,2},{2,3},{3,0},{4,5},{5,6},{6,7},{7,4},{8,9},{9,10},{10,1... | collective-permute-start | bytes 1376264 | tf_op jit(solution)/shard_map/ppermute | solution.py:103
  96.2 14.8 %collective-permute-start.3 = (bf16[32,7168]{1,0:T(8,128)(2,1)S(1)}, bf16[32,7168]{1,0:T(8,128)(2,1)S(1)}, u32[]{:S(2)}, u32[]{:S(2)}) collective-permute-start(bf16[32,7168]{1,0:T(8,128)(2,1)S(1)} %get-tuple-element.37), channel_id=1, source_target_pairs={{0,4},{4,0},{8,12},{12,8},{16,20},{20,16},{24,28},{28,24},{32,36},... | collective-permute-start | bytes 1376264 | tf_op jit(solution)/shard_map/ppermute | solution.py:100
  96.2 14.8 %collective-permute-start.2 = (bf16[32,7168]{1,0:T(8,128)(2,1)S(1)}, bf16[32,7168]{1,0:T(8,128)(2,1)S(1)}, u32[]{:S(2)}, u32[]{:S(2)}) collective-permute-start(bf16[32,7168]{1,0:T(8,128)(2,1)S(1)} %get-tuple-element.36), channel_id=1, source_target_pairs={{0,4},{4,0},{8,12},{12,8},{16,20},{20,16},{24,28},{28,24},{32,36},... | collective-permute-start | bytes 1376264 | tf_op jit(solution)/shard_map/ppermute | solution.py:100
  107.7 12.0 %collective-permute-start.29 = (bf16[32,7168]{1,0:T(8,128)(2,1)S(1)}, bf16[32,7168]{1,0:T(8,128)(2,1)S(1)}, u32[]{:S(2)}, u32[]{:S(2)}) collective-permute-start(bf16[32,7168]{1,0:T(8,128)(2,1)S(1)} %get-tuple-element.60), channel_id=1, source_target_pairs={{0,1},{1,2},{2,3},{3,0},{4,5},{5,6},{6,7},{7,4},{8,9},{9,10},{10,1... | collective-permute-start | bytes 1376264 | tf_op jit(solution)/shard_map/ppermute | solution.py:103
  108.0 11.7 %collective-permute-start.31 = (bf16[32,7168]{1,0:T(8,128)(2,1)S(1)}, bf16[32,7168]{1,0:T(8,128)(2,1)S(1)}, u32[]{:S(2)}, u32[]{:S(2)}) collective-permute-start(bf16[32,7168]{1,0:T(8,128)(2,1)S(1)} %get-tuple-element.59), channel_id=1, source_target_pairs={{0,3},{1,0},{2,1},{3,2},{4,7},{5,4},{6,5},{7,6},{8,11},{9,8},{10,9... | collective-permute-start | bytes 1376264 | tf_op jit(solution)/shard_map/ppermute | solution.py:103
  121.5 6.0 %copy-start.4 = (s32[4,8]{1,0:T(4,128)S(1)}, s32[4,8]{1,0:T(4,128)}, u32[]{:S(2)}) copy-start(s32[4,8]{1,0:T(4,128)} %param.7) | copy-start | bytes 388
  121.5 28.6 %all-to-all-start.1 = ((bf16[32,2,7168]{2,1,0:T(2,128)(2,1)}), bf16[32,2,7168]{2,1,0:T(2,128)(2,1)S(1)}, u32[]{:S(2)}, u32[]{:S(2)}) async-start(bf16[32,2,7168]{2,1,0:T(2,128)(2,1)} %all_to_all.14), calls=%async_computation.1 | async-start | bytes 1835008 | tf_op jit(solution)/shard_map/all_to_all | solution.py:108

commit v3 on v2

--- a/solution.py
+++ b/solution.py
@@ -24,6 +24,19 @@
         compiler_params=pltpu.CompilerParams(vmem_limit_bytes=MIB),
         cost_estimate=pl.CostEstimate(flops=cost * 64, bytes_accessed=cost, transcendentals=0),
     )(*values, *first)
+
+
+def taken(value, *first):
+    def kernel(*refs):
+        refs[-1][...] = refs[0][...]
+
+    return pl.pallas_call(
+        kernel,
+        in_specs=[ONCHIP] + [ANYWHERE] * len(first),
+        out_specs=ONCHIP,
+        out_shape=jax.ShapeDtypeStruct(value.shape, value.dtype),
+        compiler_params=pltpu.CompilerParams(vmem_limit_bytes=MIB),
+    )(value, *first)
 
 
 def stage_kernel(*refs):
@@ -163,7 +176,7 @@
     from_right = wide(jnp.concatenate([to_left, last_left], axis=0))
     own_total = wide(own_kept) + wide(own_got)
     returned = exchange(narrow(own_total + from_left + from_right))
-    (affinity,) = after([affinity], own_kept)
+    affinity = taken(affinity, own_kept)
     weights = 2.5 * affinity / jnp.sum(affinity, axis=1, keepdims=True)
     shares = jnp.sum(matches * weights[:, :, None], axis=1)
     coefficients = picked * jnp.repeat(shares.T, slots, axis=0)

time: 152 us -> 151 us (level)
    unnamed x11 -> x12, local copies, waits for them, and re-layouts: 6.81 us -> 6.13 us
where the time goes in v3:
time: 151 us
  waiting for transfers between devices  64.3 us (43%)
  blocking collectives  36.7 us (24%)
  starting transfers between devices  28.5 us (19%)
  local copies, waits for them, and re-layouts  9.26 us (6%)
  Pallas kernels  7.51 us (5%)
  other arithmetic  2.37 us (2%)
  matrix products  1.61 us (1%)
    ppermute x12, waiting for transfers between devices, over_y(): lax.ppermute(value, 'tp', [(i, (i + shift) % tp_count) for i in range(tp_...  36.9 us
    all_to_all x1, blocking collectives, exchange(): lax.all_to_all(value, 'ep', split_axis=0, concat_axis=0, axis_index_group...  36.7 us
    all_to_all x1, waiting for transfers between devices, exchange(): lax.all_to_all(value, 'ep', split_axis=0, concat_axis=0, axis_index_group...  22.4 us
    ppermute x12, starting transfers between devices, over_y(): lax.ppermute(value, 'tp', [(i, (i + shift) % tp_count) for i in range(tp_...  17.9 us
    pallas_call x3, Pallas kernels, ffn(): pl.pallas_call(functools.partial(ffn_kernel, len(own), len(other), 4), in...  6.74 us
    unnamed x12, local copies, waits for them, and re-layouts  6.13 us
    all_to_all x1, starting transfers between devices, exchange(): lax.all_to_all(value, 'ep', split_axis=0, concat_axis=0, axis_index_group...  5.68 us
    ppermute x20, waiting for transfers between devices, over_core(): return lax.ppermute(value, 'ep', [(i, i ^ 1) for i in range(ep_count)])  4.99 us
  transfers between devices with their start and end apart: 33, of which 18 were waited for; matrix products, arithmetic and copies ran while one was open for 1% of the time, Pallas kernels for 5%

profile of v3, /device:TPU:2, one launch (start us, length us, event | category | flops | bytes accessed | tf_op | source)
XLA Modules:
  0.0 150.5 jit_solution(3634547650948746403)
XLA Ops:
  0.0 0.8 convert_reduce_fusion
  1.2 0.4 convolution_convert_fusion
  1.6 0.3 all_to_all.12
  2.0 36.7 %all_to_all.18 = bf16[32,2,7168]{2,1,0:T(2,128)(2,1)S(1)} all-to-all(bf16[32,2,7168]{2,1,0:T(2,128)(2,1)S(1)} %all_to_all.12), channel_id=1, replica_groups={{0,8,16,24,32,40,48,56,64,72,80,88,96,104,112,120,128,136,144,152,160,1..., dimensions={0} | all-to-all | bytes 1835008 | tf_op jit(solution)/shard_map/all_to_all | solution.py:121
  38.6 0.6 fusion.7
  39.7 0.6 collective-permute-start.1
  40.3 1.6 %collective-permute-start.4 = (bf16[32,7168]{1,0:T(8,128)(2,1)S(1)}, bf16[32,7168]{1,0:T(8,128)(2,1)S(1)}, u32[]{:S(2)}, u32[]{:S(2)}) collective-permute-start(bf16[32,7168]{1,0:T(8,128)(2,1)S(1)} %slice.55.refs_0_), channel_id=1, source_target_pairs={{0,1},{1,2},{2,3},{3,0},{4,5},{5,6},{6,7},{7,4},{8,9},{9,10},{10,1... | collective-permute-start | bytes 1376264 | tf_op jit(solution)/shard_map/ppermute | solution.py:116
  41.9 1.7 %collective-permute-start.5 = (bf16[32,7168]{1,0:T(8,128)(2,1)S(1)}, bf16[32,7168]{1,0:T(8,128)(2,1)S(1)}, u32[]{:S(2)}, u32[]{:S(2)}) collective-permute-start(bf16[32,7168]{1,0:T(8,128)(2,1)S(1)} %slice.57.refs_1_), channel_id=1, source_target_pairs={{0,3},{1,0},{2,1},{3,2},{4,7},{5,4},{6,5},{7,6},{8,11},{9,8},{10,9... | collective-permute-start | bytes 1376264 | tf_op jit(solution)/shard_map/ppermute | solution.py:116
  43.5 2.0 %copy-done.1 = bf16[1,7168,256]{2,1,0:T(8,128)(2,1)S(1)} copy-done((bf16[1,7168,256]{2,1,0:T(8,128)(2,1)S(1)}, bf16[1,7168,256]{2,1,0:T(8,128)(2,1)}, u32[]{:S(2)}) %copy-start.1) | copy-done | bytes 3670040
  45.6 2.0 %copy-done.2 = bf16[1,7168,256]{2,1,0:T(8,128)(2,1)S(1)} copy-done((bf16[1,7168,256]{2,1,0:T(8,128)(2,1)S(1)}, bf16[1,7168,256]{2,1,0:T(8,128)(2,1)}, u32[]{:S(2)}) %copy-start.2) | copy-done | bytes 3670040
  47.6 2.0 %copy-done.3 = bf16[1,256,7168]{2,1,0:T(8,128)(2,1)S(1)} copy-done((bf16[1,256,7168]{2,1,0:T(8,128)(2,1)S(1)}, bf16[1,256,7168]{2,1,0:T(8,128)(2,1)}, u32[]{:S(2)}) %copy-start.3) | copy-done | bytes 3670040
  49.7 0.8 shard_map.64
  50.4 0.4 collective-permute-start.6
  50.9 2.9 %collective-permute-start.7 = (bf16[32,7168]{1,0:T(8,128)(2,1)S(1)}, bf16[32,7168]{1,0:T(8,128)(2,1)S(1)}, u32[]{:S(2)}, u32[]{:S(2)}) collective-permute-start(bf16[32,7168]{1,0:T(8,128)(2,1)S(1)} %slice.55.refs_0_), channel_id=1, source_target_pairs={{0,3},{1,0},{2,1},{3,2},{4,7},{5,4},{6,5},{7,6},{8,11},{9,8},{10,9... | collective-permute-start | bytes 1376264 | tf_op jit(solution)/shard_map/ppermute | solution.py:116
  53.8 1.8 %shard_map.65 = (bf16[64,7168]{1,0:T(8,128)(2,1)S(1)}, bf16[32,7168]{1,0:T(8,128)(2,1)S(1)}, bf16[32,7168]{1,0:T(8,128)(2,1)S(1)}) custom-call(bf16[32,7168]{1,0:T(8,128)(2,1)S(1)} %slice.55.refs_0_, bf16[32,7168]{1,0:T(8,128)(2,1)S(1)} %slice.57.refs_1_, bf16[32,7168]{1,0:T(8,128)(2,1)S(1)} %collective-permute-done.refs_2_, ...), custom_call_target="tpu_custom_call" | custom-call | tf_op jit(solution)/shard_map/pallas_call | solution.py:90
  55.6 1.3 collective-permute-start.20
  57.0 2.0 %collective-permute-start.21 = (bf16[32,7168]{1,0:T(8,128)(2,1)S(1)}, bf16[32,7168]{1,0:T(8,128)(2,1)S(1)}, u32[]{:S(2)}, u32[]{:S(2)}) collective-permute-start(bf16[32,7168]{1,0:T(8,128)(2,1)S(1)} %get-tuple-element.39.refs_1_), channel_id=1, source_target_pairs={{0,3},{1,0},{2,1},{3,2},{4,7},{5,4},{6,5},{7,6},{8,11},{9,8},{10,9... | collective-permute-start | bytes 1376264 | tf_op jit(solution)/shard_map/ppermute | solution.py:116
  59.1 6.1 %collective-permute-done.6.refs_2_ = bf16[32,7168]{1,0:T(8,128)(2,1)S(1)} collective-permute-done((bf16[32,7168]{1,0:T(8,128)(2,1)S(1)}, bf16[32,7168]{1,0:T(8,128)(2,1)S(1)}, u32[]{:S(2)}, u32[]{:S(2)}) %collective-permute-start.6) | collective-permute-done | bytes 458784 | tf_op jit(solution)/shard_map/ppermute | solution.py:116
  65.2 0.6 collective-permute-start.10
  66.1 0.6 collective-permute-done.9.refs_5_
  67.6 0.5 collective-permute-done.12.refs_8_
  68.5 0.3 collective-permute-done.14.refs_10_
  68.8 0.8 collective-permute-done.15.refs_11_
  69.6 3.1 %shard_map.68 = (bf16[128,7168]{1,0:T(8,128)(2,1)S(1)}, bf16[32,7168]{1,0:T(8,128)(2,1)S(1)}, bf16[32,7168]{1,0:T(8,128)(2,1)S(1)}, bf16[32,7168]{1,0:T(8,128)(2,1)S(1)}, bf16[32,7168]{1,0:T(8,128)(2,1)S(1)}) custom-call(bf16[32,7168]{1,0:T(8,128)(2,1)S(1)} %get-tuple-element.38.refs_0_, bf16[32,7168]{1,0:T(8,128)(2,1)S(1)} %get-tuple-element.39.refs_1_, ...), custom_call_target="tpu_custom_call" | custom-call | tf_op jit(solution)/shard_map/pallas_call | solution.py:90
  73.0 0.4 collective-permute-start.17
  73.9 0.4 collective-permute-start.23
  74.3 0.4 collective-permute-done.16.refs_0_
  74.7 0.7 collective-permute-done.17.refs_1_
  75.3 0.7 collective-permute-done.18.refs_2_
  76.0 0.7 collective-permute-done.19.refs_3_
  77.0 2.6 %collective-permute-start.26 = (bf16[32,7168]{1,0:T(8,128)(2,1)S(1)}, bf16[32,7168]{1,0:T(8,128)(2,1)S(1)}, u32[]{:S(2)}, u32[]{:S(2)}) collective-permute-start(bf16[32,7168]{1,0:T(8,128)(2,1)S(1)} %get-tuple-element.62), channel_id=1, source_target_pairs={{0,3},{1,0},{2,1},{3,2},{4,7},{5,4},{6,5},{7,6},{8,11},{9,8},{10,9... | collective-permute-start | bytes 1376264 | tf_op jit(solution)/shard_map/ppermute | solution.py:116
  79.6 1.8 %shard_map.71 = (bf16[64,7168]{1,0:T(8,128)(2,1)S(1)}, bf16[32,7168]{1,0:T(8,128)(2,1)S(1)}, bf16[32,7168]{1,0:T(8,128)(2,1)S(1)}) custom-call(bf16[32,7168]{1,0:T(8,128)(2,1)S(1)} %get-tuple-element.48.refs_0_, bf16[32,7168]{1,0:T(8,128)(2,1)S(1)} %get-tuple-element.46.refs_5_.refs_1_, bf16[32,7168]{1,0:T(8,128)(2,1)S(1)} %collective-permute-done.22.refs_2_, ...), custom_call_target="tpu_custom_call" | custom-call | tf_op jit(solution)/shard_map/pallas_call | solution.py:90
  81.5 0.5 collective-permute-start.25
  82.0 7.9 %collective-permute-done.26.refs_0_ = bf16[32,7168]{1,0:T(8,128)(2,1)S(1)} collective-permute-done((bf16[32,7168]{1,0:T(8,128)(2,1)S(1)}, bf16[32,7168]{1,0:T(8,128)(2,1)S(1)}, u32[]{:S(2)}, u32[]{:S(2)}) %collective-permute-start.26) | collective-permute-done | bytes 458784 | tf_op jit(solution)/shard_map/ppermute | solution.py:116
  89.9 3.4 %collective-permute-done.27.refs_1_ = bf16[32,7168]{1,0:T(8,128)(2,1)S(1)} collective-permute-done((bf16[32,7168]{1,0:T(8,128)(2,1)S(1)}, bf16[32,7168]{1,0:T(8,128)(2,1)S(1)}, u32[]{:S(2)}, u32[]{:S(2)}) %collective-permute-start.27) | collective-permute-done | bytes 458784 | tf_op jit(solution)/shard_map/ppermute | solution.py:116
  93.5 0.4 collective-permute-start.30
  93.9 1.7 %collective-permute-start.28 = (bf16[32,7168]{1,0:T(8,128)(2,1)S(1)}, bf16[32,7168]{1,0:T(8,128)(2,1)S(1)}, u32[]{:S(2)}, u32[]{:S(2)}) collective-permute-start(bf16[32,7168]{1,0:T(8,128)(2,1)S(1)} %get-tuple-element.64), channel_id=1, source_target_pairs={{0,1},{1,2},{2,3},{3,0},{4,5},{5,6},{6,7},{7,4},{8,9},{9,10},{10,1... | collective-permute-start | bytes 1376264 | tf_op jit(solution)/shard_map/ppermute | solution.py:116
  95.6 0.5 collective-permute-start.2
  96.1 9.1 %collective-permute-done.30 = bf16[32,7168]{1,0:T(8,128)(2,1)S(1)} collective-permute-done((bf16[32,7168]{1,0:T(8,128)(2,1)S(1)}, bf16[32,7168]{1,0:T(8,128)(2,1)S(1)}, u32[]{:S(2)}, u32[]{:S(2)}) %collective-permute-start.30) | collective-permute-done | bytes 458784 | tf_op jit(solution)/shard_map/ppermute | solution.py:116
  105.2 1.5 %collective-permute-done.28 = bf16[32,7168]{1,0:T(8,128)(2,1)S(1)} collective-permute-done((bf16[32,7168]{1,0:T(8,128)(2,1)S(1)}, bf16[32,7168]{1,0:T(8,128)(2,1)S(1)}, u32[]{:S(2)}, u32[]{:S(2)}) %collective-permute-start.28) | collective-permute-done | bytes 458784 | tf_op jit(solution)/shard_map/ppermute | solution.py:116
  106.7 0.3 add_convert_fusion.1
  107.4 3.0 %collective-permute-start.31 = (bf16[32,7168]{1,0:T(8,128)(2,1)S(1)}, bf16[32,7168]{1,0:T(8,128)(2,1)S(1)}, u32[]{:S(2)}, u32[]{:S(2)}) collective-permute-start(bf16[32,7168]{1,0:T(8,128)(2,1)S(1)} %get-tuple-element.59), channel_id=1, source_target_pairs={{0,3},{1,0},{2,1},{3,2},{4,7},{5,4},{6,5},{7,6},{8,11},{9,8},{10,9... | collective-permute-start | bytes 1376264 | tf_op jit(solution)/shard_map/ppermute | solution.py:116
  110.4 8.7 %collective-permute-done.29 = bf16[32,7168]{1,0:T(8,128)(2,1)S(1)} collective-permute-done((bf16[32,7168]{1,0:T(8,128)(2,1)S(1)}, bf16[32,7168]{1,0:T(8,128)(2,1)S(1)}, u32[]{:S(2)}, u32[]{:S(2)}) %collective-permute-start.29) | collective-permute-done | bytes 458784 | tf_op jit(solution)/shard_map/ppermute | solution.py:116
  119.1 0.5 add_convert_fusion
  119.6 1.3 all_to_all.14
  120.8 5.7 %all-to-all-start.1 = ((bf16[32,2,7168]{2,1,0:T(2,128)(2,1)}), bf16[32,2,7168]{2,1,0:T(2,128)(2,1)S(1)}, u32[]{:S(2)}, u32[]{:S(2)}) async-start(bf16[32,2,7168]{2,1,0:T(2,128)(2,1)} %all_to_all.14), calls=%async_computation.1 | async-start | bytes 1835008 | tf_op jit(solution)/shard_map/all_to_all | solution.py:121
  127.0 22.4 %all-to-all-done.1 = bf16[32,2,7168]{2,1,0:T(2,128)(2,1)S(1)} async-done(((bf16[32,2,7168]{2,1,0:T(2,128)(2,1)}), bf16[32,2,7168]{2,1,0:T(2,128)(2,1)S(1)}, u32[]{:S(2)}, u32[]{:S(2)}) %all-to-all-start.1) | async-done | bytes 917536 | tf_op jit(solution)/shard_map/all_to_all | solution.py:121
  149.3 1.2 fusion
  (70 shorter events, 4.7 us)
Async XLA Ops:
  0.0 1.2 copy-start
  39.4 11.4 %collective-permute-start = (bf16[32,7168]{1,0:T(8,128)(2,1)S(1)}, bf16[32,7168]{1,0:T(8,128)(2,1)S(1)}, u32[]{:S(2)}, u32[]{:S(2)}) collective-permute-start(bf16[32,7168]{1,0:T(8,128)(2,1)S(1)} %slice.55.refs_0_), channel_id=1, source_target_pairs={{0,4},{4,0},{8,12},{12,8},{16,20},{20,16},{24,28},{28,24},{32,36},... | collective-permute-start | bytes 1376264 | tf_op jit(solution)/shard_map/ppermute | solution.py:113
  39.7 14.0 %collective-permute-start.1 = (bf16[32,7168]{1,0:T(8,128)(2,1)S(1)}, bf16[32,7168]{1,0:T(8,128)(2,1)S(1)}, u32[]{:S(2)}, u32[]{:S(2)}) collective-permute-start(bf16[32,7168]{1,0:T(8,128)(2,1)S(1)} %slice.57.refs_1_), channel_id=1, source_target_pairs={{0,4},{4,0},{8,12},{12,8},{16,20},{20,16},{24,28},{28,24},{32,36},... | collective-permute-start | bytes 1376264 | tf_op jit(solution)/shard_map/ppermute | solution.py:113
  40.3 15.3 %collective-permute-start.4 = (bf16[32,7168]{1,0:T(8,128)(2,1)S(1)}, bf16[32,7168]{1,0:T(8,128)(2,1)S(1)}, u32[]{:S(2)}, u32[]{:S(2)}) collective-permute-start(bf16[32,7168]{1,0:T(8,128)(2,1)S(1)} %slice.55.refs_0_), channel_id=1, source_target_pairs={{0,1},{1,2},{2,3},{3,0},{4,5},{5,6},{6,7},{7,4},{8,9},{9,10},{10,1... | collective-permute-start | bytes 1376264 | tf_op jit(solution)/shard_map/ppermute | solution.py:116
  41.9 13.7 %collective-permute-start.5 = (bf16[32,7168]{1,0:T(8,128)(2,1)S(1)}, bf16[32,7168]{1,0:T(8,128)(2,1)S(1)}, u32[]{:S(2)}, u32[]{:S(2)}) collective-permute-start(bf16[32,7168]{1,0:T(8,128)(2,1)S(1)} %slice.57.refs_1_), channel_id=1, source_target_pairs={{0,3},{1,0},{2,1},{3,2},{4,7},{5,4},{6,5},{7,6},{8,11},{9,8},{10,9... | collective-permute-start | bytes 1376264 | tf_op jit(solution)/shard_map/ppermute | solution.py:116
  43.5 2.0 %copy-start.1 = (bf16[1,7168,256]{2,1,0:T(8,128)(2,1)S(1)}, bf16[1,7168,256]{2,1,0:T(8,128)(2,1)}, u32[]{:S(2)}) copy-start(bf16[1,7168,256]{2,1,0:T(8,128)(2,1)} %refs_0_.2) | copy-start | bytes 11010052
  45.6 2.0 %copy-start.2 = (bf16[1,7168,256]{2,1,0:T(8,128)(2,1)S(1)}, bf16[1,7168,256]{2,1,0:T(8,128)(2,1)}, u32[]{:S(2)}) copy-start(bf16[1,7168,256]{2,1,0:T(8,128)(2,1)} %refs_1_.1) | copy-start | bytes 11010052
  47.6 2.0 %copy-start.3 = (bf16[1,256,7168]{2,1,0:T(8,128)(2,1)S(1)}, bf16[1,256,7168]{2,1,0:T(8,128)(2,1)}, u32[]{:S(2)}) copy-start(bf16[1,256,7168]{2,1,0:T(8,128)(2,1)} %refs_2_.1) | copy-start | bytes 11010052
  50.4 14.7 %collective-permute-start.6 = (bf16[32,7168]{1,0:T(8,128)(2,1)S(1)}, bf16[32,7168]{1,0:T(8,128)(2,1)S(1)}, u32[]{:S(2)}, u32[]{:S(2)}) collective-permute-start(bf16[32,7168]{1,0:T(8,128)(2,1)S(1)} %slice.57.refs_1_), channel_id=1, source_target_pairs={{0,1},{1,2},{2,3},{3,0},{4,5},{5,6},{6,7},{7,4},{8,9},{9,10},{10,1... | collective-permute-start | bytes 1376264 | tf_op jit(solution)/shard_map/ppermute | solution.py:116
  50.9 14.3 %collective-permute-start.7 = (bf16[32,7168]{1,0:T(8,128)(2,1)S(1)}, bf16[32,7168]{1,0:T(8,128)(2,1)S(1)}, u32[]{:S(2)}, u32[]{:S(2)}) collective-permute-start(bf16[32,7168]{1,0:T(8,128)(2,1)S(1)} %slice.55.refs_0_), channel_id=1, source_target_pairs={{0,3},{1,0},{2,1},{3,2},{4,7},{5,4},{6,5},{7,6},{8,11},{9,8},{10,9... | collective-permute-start | bytes 1376264 | tf_op jit(solution)/shard_map/ppermute | solution.py:116
  55.6 18.1 %collective-permute-start.20 = (bf16[32,7168]{1,0:T(8,128)(2,1)S(1)}, bf16[32,7168]{1,0:T(8,128)(2,1)S(1)}, u32[]{:S(2)}, u32[]{:S(2)}) collective-permute-start(bf16[32,7168]{1,0:T(8,128)(2,1)S(1)} %get-tuple-element.38.refs_0_), channel_id=1, source_target_pairs={{0,1},{1,2},{2,3},{3,0},{4,5},{5,6},{6,7},{7,4},{8,9},{9,10},{10,1... | collective-permute-start | bytes 1376264 | tf_op jit(solution)/shard_map/ppermute | solution.py:116
  57.0 16.9 %collective-permute-start.21 = (bf16[32,7168]{1,0:T(8,128)(2,1)S(1)}, bf16[32,7168]{1,0:T(8,128)(2,1)S(1)}, u32[]{:S(2)}, u32[]{:S(2)}) collective-permute-start(bf16[32,7168]{1,0:T(8,128)(2,1)S(1)} %get-tuple-element.39.refs_1_), channel_id=1, source_target_pairs={{0,3},{1,0},{2,1},{3,2},{4,7},{5,4},{6,5},{7,6},{8,11},{9,8},{10,9... | collective-permute-start | bytes 1376264 | tf_op jit(solution)/shard_map/ppermute | solution.py:116
  59.1 6.7 %collective-permute-start.8 = (bf16[16,7168]{1,0:T(8,128)(2,1)S(1)}, bf16[16,7168]{1,0:T(8,128)(2,1)S(1)}, u32[]{:S(2)}, u32[]{:S(2)}) collective-permute-start(bf16[16,7168]{1,0:T(8,128)(2,1)S(1)} %get-tuple-element.74), channel_id=1, source_target_pairs={{0,4},{4,0},{8,12},{12,8},{16,20},{20,16},{24,28},{28,24},{32,36},... | collective-permute-start | bytes 688136 | tf_op jit(solution)/shard_map/ppermute | solution.py:113
  65.2 1.5 collective-permute-start.9
  65.2 1.8 %collective-permute-start.10 = (bf16[16,7168]{1,0:T(8,128)(2,1)S(1)}, bf16[16,7168]{1,0:T(8,128)(2,1)S(1)}, u32[]{:S(2)}, u32[]{:S(2)}) collective-permute-start(bf16[16,7168]{1,0:T(8,128)(2,1)S(1)} %get-tuple-element.72), channel_id=1, source_target_pairs={{0,4},{4,0},{8,12},{12,8},{16,20},{20,16},{24,28},{28,24},{32,36},... | collective-permute-start | bytes 688136 | tf_op jit(solution)/shard_map/ppermute | solution.py:113
  65.8 1.5 collective-permute-start.11
  66.6 1.5 collective-permute-start.12
  67.0 1.5 collective-permute-start.13
  67.3 1.5 collective-permute-start.14
  68.1 1.5 collective-permute-start.15
  72.8 1.9 %collective-permute-start.16 = (bf16[32,7168]{1,0:T(8,128)(2,1)S(1)}, bf16[32,7168]{1,0:T(8,128)(2,1)S(1)}, u32[]{:S(2)}, u32[]{:S(2)}) collective-permute-start(bf16[32,7168]{1,0:T(8,128)(2,1)S(1)} %get-tuple-element.41), channel_id=1, source_target_pairs={{0,4},{4,0},{8,12},{12,8},{16,20},{20,16},{24,28},{28,24},{32,36},... | collective-permute-start | bytes 1376264 | tf_op jit(solution)/shard_map/ppermute | solution.py:113
  73.0 2.3 %collective-permute-start.17 = (bf16[32,7168]{1,0:T(8,128)(2,1)S(1)}, bf16[32,7168]{1,0:T(8,128)(2,1)S(1)}, u32[]{:S(2)}, u32[]{:S(2)}) collective-permute-start(bf16[32,7168]{1,0:T(8,128)(2,1)S(1)} %get-tuple-element.42), channel_id=1, source_target_pairs={{0,4},{4,0},{8,12},{12,8},{16,20},{20,16},{24,28},{28,24},{32,36},... | collective-permute-start | bytes 1376264 | tf_op jit(solution)/shard_map/ppermute | solution.py:113
  73.4 2.6 %collective-permute-start.18 = (bf16[32,7168]{1,0:T(8,128)(2,1)S(1)}, bf16[32,7168]{1,0:T(8,128)(2,1)S(1)}, u32[]{:S(2)}, u32[]{:S(2)}) collective-permute-start(bf16[32,7168]{1,0:T(8,128)(2,1)S(1)} %get-tuple-element.43), channel_id=1, source_target_pairs={{0,4},{4,0},{8,12},{12,8},{16,20},{20,16},{24,28},{28,24},{32,36},... | collective-permute-start | bytes 1376264 | tf_op jit(solution)/shard_map/ppermute | solution.py:113
  73.8 2.9 %collective-permute-start.19 = (bf16[32,7168]{1,0:T(8,128)(2,1)S(1)}, bf16[32,7168]{1,0:T(8,128)(2,1)S(1)}, u32[]{:S(2)}, u32[]{:S(2)}) collective-permute-start(bf16[32,7168]{1,0:T(8,128)(2,1)S(1)} %get-tuple-element.44), channel_id=1, source_target_pairs={{0,4},{4,0},{8,12},{12,8},{16,20},{20,16},{24,28},{28,24},{32,36},... | collective-permute-start | bytes 1376264 | tf_op jit(solution)/shard_map/ppermute | solution.py:113
  73.9 5.7 %collective-permute-start.23 = (bf16[32,7168]{1,0:T(8,128)(2,1)S(1)}, bf16[32,7168]{1,0:T(8,128)(2,1)S(1)}, u32[]{:S(2)}, u32[]{:S(2)}) collective-permute-start(bf16[32,7168]{1,0:T(8,128)(2,1)S(1)} %get-tuple-element.46.refs_5_.refs_1_), channel_id=1, source_target_pairs={{0,4},{4,0},{8,12},{12,8},{16,20},{20,16},{24,28},{28,24},{32,36},... | collective-permute-start | bytes 1376264 | tf_op jit(solution)/shard_map/ppermute | solution.py:113
  76.7 2.9 %collective-permute-start.22 = (bf16[32,7168]{1,0:T(8,128)(2,1)S(1)}, bf16[32,7168]{1,0:T(8,128)(2,1)S(1)}, u32[]{:S(2)}, u32[]{:S(2)}) collective-permute-start(bf16[32,7168]{1,0:T(8,128)(2,1)S(1)} %get-tuple-element.48.refs_0_), channel_id=1, source_target_pairs={{0,4},{4,0},{8,12},{12,8},{16,20},{20,16},{24,28},{28,24},{32,36},... | collective-permute-start | bytes 1376264 | tf_op jit(solution)/shard_map/ppermute | solution.py:113
  77.0 12.9 %collective-permute-start.26 = (bf16[32,7168]{1,0:T(8,128)(2,1)S(1)}, bf16[32,7168]{1,0:T(8,128)(2,1)S(1)}, u32[]{:S(2)}, u32[]{:S(2)}) collective-permute-start(bf16[32,7168]{1,0:T(8,128)(2,1)S(1)} %get-tuple-element.62), channel_id=1, source_target_pairs={{0,3},{1,0},{2,1},{3,2},{4,7},{5,4},{6,5},{7,6},{8,11},{9,8},{10,9... | collective-permute-start | bytes 1376264 | tf_op jit(solution)/shard_map/ppermute | solution.py:116
  79.6 13.7 %collective-permute-start.27 = (bf16[32,7168]{1,0:T(8,128)(2,1)S(1)}, bf16[32,7168]{1,0:T(8,128)(2,1)S(1)}, u32[]{:S(2)}, u32[]{:S(2)}) collective-permute-start(bf16[32,7168]{1,0:T(8,128)(2,1)S(1)} %get-tuple-element.61), channel_id=1, source_target_pairs={{0,1},{1,2},{2,3},{3,0},{4,5},{5,6},{6,7},{7,4},{8,9},{9,10},{10,1... | collective-permute-start | bytes 1376264 | tf_op jit(solution)/shard_map/ppermute | solution.py:116
  81.4 11.9 %collective-permute-start.24 = (bf16[32,7168]{1,0:T(8,128)(2,1)S(1)}, bf16[32,7168]{1,0:T(8,128)(2,1)S(1)}, u32[]{:S(2)}, u32[]{:S(2)}) collective-permute-start(bf16[32,7168]{1,0:T(8,128)(2,1)S(1)} %get-tuple-element.50), channel_id=1, source_target_pairs={{0,4},{4,0},{8,12},{12,8},{16,20},{20,16},{24,28},{28,24},{32,36},... | collective-permute-start | bytes 1376264 | tf_op jit(solution)/shard_map/ppermute | solution.py:113
  81.5 11.8 %collective-permute-start.25 = (bf16[32,7168]{1,0:T(8,128)(2,1)S(1)}, bf16[32,7168]{1,0:T(8,128)(2,1)S(1)}, u32[]{:S(2)}, u32[]{:S(2)}) collective-permute-start(bf16[32,7168]{1,0:T(8,128)(2,1)S(1)} %get-tuple-element.51), channel_id=1, source_target_pairs={{0,4},{4,0},{8,12},{12,8},{16,20},{20,16},{24,28},{28,24},{32,36},... | collective-permute-start | bytes 1376264 | tf_op jit(solution)/shard_map/ppermute | solution.py:113
  93.5 11.7 %collective-permute-start.30 = (bf16[32,7168]{1,0:T(8,128)(2,1)S(1)}, bf16[32,7168]{1,0:T(8,128)(2,1)S(1)}, u32[]{:S(2)}, u32[]{:S(2)}) collective-permute-start(bf16[32,7168]{1,0:T(8,128)(2,1)S(1)} %get-tuple-element.63), channel_id=1, source_target_pairs={{0,3},{1,0},{2,1},{3,2},{4,7},{5,4},{6,5},{7,6},{8,11},{9,8},{10,9... | collective-permute-start | bytes 1376264 | tf_op jit(solution)/shard_map/ppermute | solution.py:116
  93.9 12.9 %collective-permute-start.28 = (bf16[32,7168]{1,0:T(8,128)(2,1)S(1)}, bf16[32,7168]{1,0:T(8,128)(2,1)S(1)}, u32[]{:S(2)}, u32[]{:S(2)}) collective-permute-start(bf16[32,7168]{1,0:T(8,128)(2,1)S(1)} %get-tuple-element.64), channel_id=1, source_target_pairs={{0,1},{1,2},{2,3},{3,0},{4,5},{5,6},{6,7},{7,4},{8,9},{9,10},{10,1... | collective-permute-start | bytes 1376264 | tf_op jit(solution)/shard_map/ppermute | solution.py:116
  95.6 14.8 %collective-permute-start.3 = (bf16[32,7168]{1,0:T(8,128)(2,1)S(1)}, bf16[32,7168]{1,0:T(8,128)(2,1)S(1)}, u32[]{:S(2)}, u32[]{:S(2)}) collective-permute-start(bf16[32,7168]{1,0:T(8,128)(2,1)S(1)} %get-tuple-element.37), channel_id=1, source_target_pairs={{0,4},{4,0},{8,12},{12,8},{16,20},{20,16},{24,28},{28,24},{32,36},... | collective-permute-start | bytes 1376264 | tf_op jit(solution)/shard_map/ppermute | solution.py:113
  95.6 14.8 %collective-permute-start.2 = (bf16[32,7168]{1,0:T(8,128)(2,1)S(1)}, bf16[32,7168]{1,0:T(8,128)(2,1)S(1)}, u32[]{:S(2)}, u32[]{:S(2)}) collective-permute-start(bf16[32,7168]{1,0:T(8,128)(2,1)S(1)} %get-tuple-element.36), channel_id=1, source_target_pairs={{0,4},{4,0},{8,12},{12,8},{16,20},{20,16},{24,28},{28,24},{32,36},... | collective-permute-start | bytes 1376264 | tf_op jit(solution)/shard_map/ppermute | solution.py:113
  107.1 12.0 %collective-permute-start.29 = (bf16[32,7168]{1,0:T(8,128)(2,1)S(1)}, bf16[32,7168]{1,0:T(8,128)(2,1)S(1)}, u32[]{:S(2)}, u32[]{:S(2)}) collective-permute-start(bf16[32,7168]{1,0:T(8,128)(2,1)S(1)} %get-tuple-element.60), channel_id=1, source_target_pairs={{0,1},{1,2},{2,3},{3,0},{4,5},{5,6},{6,7},{7,4},{8,9},{9,10},{10,1... | collective-permute-start | bytes 1376264 | tf_op jit(solution)/shard_map/ppermute | solution.py:116
  107.4 11.7 %collective-permute-start.31 = (bf16[32,7168]{1,0:T(8,128)(2,1)S(1)}, bf16[32,7168]{1,0:T(8,128)(2,1)S(1)}, u32[]{:S(2)}, u32[]{:S(2)}) collective-permute-start(bf16[32,7168]{1,0:T(8,128)(2,1)S(1)} %get-tuple-element.59), channel_id=1, source_target_pairs={{0,3},{1,0},{2,1},{3,2},{4,7},{5,4},{6,5},{7,6},{8,11},{9,8},{10,9... | collective-permute-start | bytes 1376264 | tf_op jit(solution)/shard_map/ppermute | solution.py:116
  119.5 7.0 %copy-start.4 = (f32[4,8]{1,0:T(4,128)S(1)}, f32[4,8]{1,0:T(4,128)}, u32[]{:S(2)}) copy-start(f32[4,8]{1,0:T(4,128)} %refs_0_.3) | copy-start | bytes 388
  120.8 5.9 %copy-start.5 = (s32[4,8]{1,0:T(4,128)S(1)}, s32[4,8]{1,0:T(4,128)}, u32[]{:S(2)}) copy-start(s32[4,8]{1,0:T(4,128)} %param.7) | copy-start | bytes 388
  120.8 28.5 %all-to-all-start.1 = ((bf16[32,2,7168]{2,1,0:T(2,128)(2,1)}), bf16[32,2,7168]{2,1,0:T(2,128)(2,1)S(1)}, u32[]{:S(2)}, u32[]{:S(2)}) async-start(bf16[32,2,7168]{2,1,0:T(2,128)(2,1)} %all_to_all.14), calls=%async_computation.1 | async-start | bytes 1835008 | tf_op jit(solution)/shard_map/all_to_all | solution.py:121
